TPU v7x, 128 devices: a whole 4x4x4 slice. The times are simulated.
128 devices in a mesh: ctx: 32 (over y, x_hi, z), tp: 4 (over x_lo, core).
Axes of the slice: x: 4 (x_hi: 2, x_lo: 2; x = x_hi * 2 + x_lo), y: 4, z: 4, core: 2. Of those that a mesh axis runs over, the one named last changes fastest.
Arguments:
- layer_input: bfloat16 [1, 4096, 768], P(None, 'ctx'), may hold values from -6 to 6
- attention_gain: bfloat16 [2, 768], replicated, may hold values from 0.5 to 1.5
- attention_shift: bfloat16 [2, 768], replicated, may hold values from -3 to 3
- feedforward_gain: bfloat16 [2, 768], replicated, may hold values from 0.5 to 1.5
- feedforward_shift: bfloat16 [2, 768], replicated, may hold values from -3 to 3
- query_key_value_weight: bfloat16 [2, 768, 3, 768], P(None, None, None, 'tp'), may hold values from -0.21875 to 0.21875
- query_key_value_bias: bfloat16 [2, 3, 768], P(None, None, 'tp'), may hold values from -2 to 2
- attention_out_weight: bfloat16 [2, 768, 768], P(None, 'tp'), may hold values from -1.75 to 1.75
- dense_bias: bfloat16 [2, 768], replicated, may hold values from -3 to 3
- expand_weight: bfloat16 [2, 768, 3072], P(None, None, 'tp'), may hold values from -0.21875 to 0.21875
- expand_bias: bfloat16 [2, 3072], P(None, 'tp'), may hold values from -3 to 3
- down_weight: bfloat16 [2, 3072, 768], P(None, 'tp'), may hold values from -0.109375 to 0.109375
- down_bias: bfloat16 [2, 768], replicated, may hold values from -3 to 3
- output_grad: bfloat16 [1, 4096, 768], P(None, 'ctx'), may hold values from -6 to 6
Outputs:
- output: bfloat16 [1, 4096, 768], P(None, 'ctx')
- input_grad: float32 [1, 4096, 768], P(None, 'ctx')
- attention_gain_grad: float32 [2, 768], replicated
- attention_shift_grad: float32 [2, 768], replicated
- feedforward_gain_grad: float32 [2, 768], replicated
- feedforward_shift_grad: float32 [2, 768], replicated
- merged_weight_grad: float32 [2, 768, 3, 768], P(None, None, None, 'tp')
- merged_bias_grad: float32 [2, 3, 768], P(None, None, 'tp')
- dense_weight_grad: float32 [2, 768, 768], P(None, 'tp')
- dense_bias_grad: float32 [2, 768], replicated
- up_weight_grad: float32 [2, 768, 3072], P(None, None, 'tp')
- up_bias_grad: float32 [2, 3072], P(None, 'tp')
- down_weight_grad: float32 [2, 3072, 768], P(None, 'tp')
- down_bias_grad: float32 [2, 768], replicated
All inputs are finite; a program needn't handle non-finite values.
Results may differ from a plain program's by a relative error of at most 0.025.
Values may be sent and summed in bfloat16 or wider, within the bound.
A program may use at most 128 MiB of HBM per device.

v0:
```python
import jax
import jax.numpy as jnp
from jax import lax
from jax.sharding import PartitionSpec as P

HD = 64
ROT = 16
LAYERS = 2


NORM_EPSILON = 1e-05
MASKED_SCORE = -1e30


def layer_norm(values, gain, shift):
    mean_value = jnp.mean(values, axis=-1, keepdims=True)
    centred = values - mean_value
    variance = jnp.mean(centred * centred, axis=-1, keepdims=True)
    return centred * lax.rsqrt(variance + NORM_EPSILON) * gain + shift


def gelu_exact(values):
    return jax.nn.gelu(values, approximate=False)


def rotary_tables(positions):
    halves = ROT // 2
    inverse = jnp.power(10000.0, -2.0 * jnp.arange(halves, dtype=jnp.float32) / ROT)
    angles = positions[:, None] * inverse[None, :]
    return (jnp.cos(angles), jnp.sin(angles))


def rotate(values, cosine, sine):
    halves = cosine.shape[-1]
    leading = values[..., :halves]
    trailing = values[..., halves : 2 * halves]
    others = values[..., 2 * halves :]
    cos_wide = cosine[:, None, :]
    sin_wide = sine[:, None, :]
    return jnp.concatenate(
        [
            leading * cos_wide - trailing * sin_wide,
            trailing * cos_wide + leading * sin_wide,
            others,
        ],
        axis=-1,
    )


def forward_attention(queries, key_value, query_pos):
    batch, rows, heads_local, head_size = queries.shape
    local_width = heads_local * head_size
    scale = head_size ** (-0.5)
    initial = (
        jnp.full((batch, heads_local, rows), MASKED_SCORE, jnp.float32),
        jnp.zeros((batch, heads_local, rows), jnp.float32),
        jnp.zeros((batch, heads_local, rows, head_size), jnp.float32),
    )
    piece = lax.all_gather(key_value, "ctx", axis=1, tiled=True)

    def update(state):
        running_max, running_sum, accum = state
        count = piece.shape[1]
        keys = piece[..., :local_width].reshape(batch, count, heads_local, head_size)
        values = piece[..., local_width:].reshape(batch, count, heads_local, head_size)
        key_pos = jnp.arange(count, dtype=jnp.int32)
        scores = (
            jnp.einsum("sqhd,skhd->shqk", queries, keys, preferred_element_type=jnp.float32) * scale
        )
        allowed = key_pos[None, :] <= query_pos[:, None]
        masked = jnp.where(allowed, scores, MASKED_SCORE)
        new_max = jnp.maximum(running_max, jnp.max(masked, axis=-1))
        weights = jnp.where(allowed, jnp.exp(scores - new_max[..., None]), 0.0)
        new_sum = jnp.sum(weights, axis=-1)
        added = jnp.einsum(
            "shqk,skhd->shqd",
            weights.astype(jnp.bfloat16),
            values,
            preferred_element_type=jnp.float32,
        )
        return (new_max, new_sum, added)

    def unchanged(state):
        return state

    running_max, running_sum, accum = lax.cond(
        jnp.int32(0) <= query_pos[-1], update, unchanged, initial
    )
    attended = (accum / running_sum[..., None]).transpose(0, 2, 1, 3)
    log_total = running_max + jnp.log(running_sum)
    return (attended, log_total)


def block_grads(queries, out_heads, log_total, delta, query_pos, piece, start, wanted):
    batch, rows, heads_local, head_size = queries.shape
    count = piece.shape[1]
    local_width = heads_local * head_size
    scale = head_size ** (-0.5)

    def compute():
        keys = piece[..., :local_width].reshape(batch, count, heads_local, head_size)
        values = piece[..., local_width:].reshape(batch, count, heads_local, head_size)
        key_pos = jnp.arange(count, dtype=jnp.int32)
        scores = (
            jnp.einsum("sqhd,skhd->shqk", queries, keys, preferred_element_type=jnp.float32) * scale
        )
        allowed = key_pos[None, :] <= query_pos[:, None]
        probs = jnp.where(allowed, jnp.exp(scores - log_total[..., None]), 0.0)
        prob_grad = jnp.einsum(
            "sqhd,skhd->shqk", out_heads, values, preferred_element_type=jnp.float32
        )
        score_grad = (probs * (prob_grad - delta[..., None])).astype(jnp.bfloat16)
        results = []
        if wanted != "keys":
            results.append(
                jnp.einsum("shqk,skhd->sqhd", score_grad, keys, preferred_element_type=jnp.float32)
                * scale
            )
        if wanted != "query":
            key_term = (
                jnp.einsum(
                    "shqk,sqhd->skhd", score_grad, queries, preferred_element_type=jnp.float32
                )
                * scale
            )
            value_term = jnp.einsum(
                "shqk,sqhd->skhd",
                probs.astype(jnp.bfloat16),
                out_heads,
                preferred_element_type=jnp.float32,
            )
            results.append(
                jnp.concatenate(
                    [
                        key_term.reshape(batch, count, local_width),
                        value_term.reshape(batch, count, local_width),
                    ],
                    axis=-1,
                )
            )
        return tuple(results)

    def skipped():
        results = []
        if wanted != "keys":
            results.append(jnp.zeros((batch, rows, heads_local, head_size), jnp.float32))
        if wanted != "query":
            results.append(jnp.zeros((batch, count, 2 * local_width), jnp.float32))
        return tuple(results)

    return lax.cond(start <= query_pos[-1], compute, skipped)


def gather_backward(queries, out_heads, log_total, delta, query_pos, key_value):
    query_grad = (
        jnp.zeros(queries.shape, jnp.float32)
        + block_grads(
            queries,
            out_heads,
            log_total,
            delta,
            query_pos,
            lax.all_gather(key_value, "ctx", axis=1, tiled=True),
            jnp.int32(0),
            "query",
        )[0]
    )
    terms = block_grads(
        queries,
        out_heads,
        log_total,
        delta,
        query_pos,
        lax.all_gather(key_value, "ctx", axis=1, tiled=True),
        jnp.int32(0),
        "keys",
    )[0]
    block_grad = lax.psum_scatter(
        terms.astype(jnp.bfloat16), "ctx", scatter_dimension=1, tiled=True
    ).astype(jnp.float32)
    return (query_grad, block_grad)


def stack_layers(entries, position):
    return jnp.stack([entry[position] for entry in entries])


def on_device(
    layer_input,
    attention_gain,
    attention_shift,
    feedforward_gain,
    feedforward_shift,
    query_key_value_weight,
    query_key_value_bias,
    attention_out_weight,
    dense_bias,
    expand_weight,
    expand_bias,
    down_weight,
    down_bias,
    output_grad,
):
    batch, rows, width = layer_input.shape
    local_width = query_key_value_weight.shape[3]
    heads_local = local_width // HD
    own_index = lax.axis_index("ctx")
    query_pos = own_index * rows + jnp.arange(rows, dtype=jnp.int32)
    cosine, sine = rotary_tables(query_pos.astype(jnp.float32))
    residual = layer_input.astype(jnp.float32)
    saved = []
    for layer_index in range(LAYERS):
        gain_one = attention_gain[layer_index].astype(jnp.float32)
        shift_one = attention_shift[layer_index].astype(jnp.float32)
        gain_two = feedforward_gain[layer_index].astype(jnp.float32)
        shift_two = feedforward_shift[layer_index].astype(jnp.float32)
        first_normalized = layer_norm(residual, gain_one, shift_one).astype(jnp.bfloat16)
        merged_projection = jnp.einsum(
            "std,dce->stce",
            first_normalized,
            query_key_value_weight[layer_index],
            preferred_element_type=jnp.float32,
        )
        merged_projection = merged_projection + query_key_value_bias[layer_index].astype(
            jnp.float32
        )
        queries = rotate(
            merged_projection[:, :, 0].reshape(batch, rows, heads_local, HD), cosine, sine
        ).astype(jnp.bfloat16)
        keys = rotate(
            merged_projection[:, :, 1].reshape(batch, rows, heads_local, HD), cosine, sine
        ).astype(jnp.bfloat16)
        values = merged_projection[:, :, 2].astype(jnp.bfloat16)
        key_value = jnp.concatenate([keys.reshape(batch, rows, local_width), values], axis=-1)
        attended, log_total = forward_attention(queries, key_value, query_pos)
        attended = attended.reshape(batch, rows, local_width)
        attention_mixture = attended.astype(jnp.bfloat16)
        second_normalized = layer_norm(residual, gain_two, shift_two).astype(jnp.bfloat16)
        hidden_before_gelu = jnp.dot(
            second_normalized, expand_weight[layer_index], preferred_element_type=jnp.float32
        )
        hidden_before_gelu = hidden_before_gelu + expand_bias[layer_index].astype(jnp.float32)
        hidden = gelu_exact(hidden_before_gelu).astype(jnp.bfloat16)
        partial_branch = jnp.dot(
            attention_mixture, attention_out_weight[layer_index], preferred_element_type=jnp.float32
        )
        partial_branch = partial_branch + jnp.dot(
            hidden, down_weight[layer_index], preferred_element_type=jnp.float32
        )
        branch_output = lax.psum(partial_branch.astype(jnp.bfloat16), "tp").astype(jnp.float32)
        saved.append(
            (
                residual,
                first_normalized,
                second_normalized,
                queries,
                key_value,
                attended,
                attention_mixture,
                log_total,
                hidden_before_gelu,
                hidden,
            )
        )
        residual = (
            residual
            + branch_output
            + dense_bias[layer_index].astype(jnp.float32)
            + down_bias[layer_index].astype(jnp.float32)
        )
    output = residual.astype(jnp.bfloat16)
    grad = output_grad.astype(jnp.float32)
    per_layer = [None] * LAYERS
    for layer_index in reversed(range(LAYERS)):
        (
            residual_in,
            first_normalized,
            second_normalized,
            queries,
            key_value,
            attended,
            attention_mixture,
            log_total,
            hidden_before_gelu,
            hidden,
        ) = saved[layer_index]
        gain_one = attention_gain[layer_index].astype(jnp.float32)
        shift_one = attention_shift[layer_index].astype(jnp.float32)
        gain_two = feedforward_gain[layer_index].astype(jnp.float32)
        shift_two = feedforward_shift[layer_index].astype(jnp.float32)
        bias_grad = jnp.sum(grad, axis=(0, 1))
        grad_low = grad.astype(jnp.bfloat16)
        dense_weight_grad = jnp.einsum(
            "stw,ste->we", attention_mixture, grad_low, preferred_element_type=jnp.float32
        )
        down_weight_grad = jnp.einsum(
            "stf,ste->fe", hidden, grad_low, preferred_element_type=jnp.float32
        )
        hidden_grad = jnp.einsum(
            "ste,fe->stf", grad_low, down_weight[layer_index], preferred_element_type=jnp.float32
        )
        gelu_back = jax.vjp(gelu_exact, hidden_before_gelu)[1]
        pre_grad = gelu_back(hidden_grad)[0].astype(jnp.bfloat16)
        up_weight_grad = jnp.einsum(
            "std,stf->df", second_normalized, pre_grad, preferred_element_type=jnp.float32
        )
        up_bias_grad = jnp.sum(pre_grad.astype(jnp.float32), axis=(0, 1))
        normed_two_grad = jnp.einsum(
            "stf,df->std", pre_grad, expand_weight[layer_index], preferred_element_type=jnp.float32
        )
        mixed_grad = jnp.einsum(
            "ste,we->stw",
            grad_low,
            attention_out_weight[layer_index],
            preferred_element_type=jnp.float32,
        ).astype(jnp.bfloat16)
        out_heads = mixed_grad.reshape(batch, rows, heads_local, HD)
        delta = jnp.sum(
            out_heads.astype(jnp.float32) * attended.reshape(batch, rows, heads_local, HD), axis=-1
        ).transpose(0, 2, 1)
        query_grad, block_grad = gather_backward(
            queries, out_heads, log_total, delta, query_pos, key_value
        )
        query_back = rotate(query_grad, cosine, -sine).reshape(batch, rows, local_width)
        key_back = rotate(
            block_grad[..., :local_width].reshape(batch, rows, heads_local, HD), cosine, -sine
        ).reshape(batch, rows, local_width)
        merged_grad = jnp.stack(
            [query_back, key_back, block_grad[..., local_width:]], axis=2
        ).astype(jnp.bfloat16)
        merged_weight_grad = jnp.einsum(
            "std,stce->dce", first_normalized, merged_grad, preferred_element_type=jnp.float32
        )
        merged_bias_grad = jnp.sum(merged_grad.astype(jnp.float32), axis=(0, 1))
        normed_one_grad = jnp.einsum(
            "stce,dce->std",
            merged_grad,
            query_key_value_weight[layer_index],
            preferred_element_type=jnp.float32,
        )
        first_sum, second_sum = (
            lax.psum(normed_one_grad.astype(jnp.bfloat16), "tp").astype(jnp.float32),
            lax.psum(normed_two_grad.astype(jnp.bfloat16), "tp").astype(jnp.float32),
        )
        norm_one_back = jax.vjp(layer_norm, residual_in, gain_one, shift_one)[1]
        norm_two_back = jax.vjp(layer_norm, residual_in, gain_two, shift_two)[1]
        input_one, gain_one_grad, shift_one_grad = norm_one_back(first_sum)
        input_two, gain_two_grad, shift_two_grad = norm_two_back(second_sum)
        grad = grad + input_one + input_two
        per_layer[layer_index] = (
            gain_one_grad,
            shift_one_grad,
            gain_two_grad,
            shift_two_grad,
            merged_weight_grad,
            merged_bias_grad,
            dense_weight_grad,
            bias_grad,
            up_weight_grad,
            up_bias_grad,
            down_weight_grad,
            bias_grad,
        )
    shares = (
        lax.psum_scatter(
            stack_layers(per_layer, 0).astype(jnp.bfloat16), "ctx", scatter_dimension=1, tiled=True
        ).astype(jnp.float32),
        lax.psum_scatter(
            stack_layers(per_layer, 1).astype(jnp.bfloat16), "ctx", scatter_dimension=1, tiled=True
        ).astype(jnp.float32),
        lax.psum_scatter(
            stack_layers(per_layer, 2).astype(jnp.bfloat16), "ctx", scatter_dimension=1, tiled=True
        ).astype(jnp.float32),
        lax.psum_scatter(
            stack_layers(per_layer, 3).astype(jnp.bfloat16), "ctx", scatter_dimension=1, tiled=True
        ).astype(jnp.float32),
        lax.psum_scatter(
            stack_layers(per_layer, 4).astype(jnp.bfloat16), "ctx", scatter_dimension=1, tiled=True
        ).astype(jnp.float32),
        lax.psum_scatter(
            stack_layers(per_layer, 5).astype(jnp.bfloat16), "ctx", scatter_dimension=2, tiled=True
        ).astype(jnp.float32),
        lax.psum_scatter(
            stack_layers(per_layer, 6).astype(jnp.bfloat16), "ctx", scatter_dimension=2, tiled=True
        ).astype(jnp.float32),
        lax.psum_scatter(
            stack_layers(per_layer, 7).astype(jnp.bfloat16), "ctx", scatter_dimension=1, tiled=True
        ).astype(jnp.float32),
        lax.psum_scatter(
            stack_layers(per_layer, 8).astype(jnp.bfloat16), "ctx", scatter_dimension=1, tiled=True
        ).astype(jnp.float32),
        lax.psum_scatter(
            stack_layers(per_layer, 9).astype(jnp.bfloat16), "ctx", scatter_dimension=1, tiled=True
        ).astype(jnp.float32),
        lax.psum_scatter(
            stack_layers(per_layer, 10).astype(jnp.bfloat16), "ctx", scatter_dimension=2, tiled=True
        ).astype(jnp.float32),
        lax.psum_scatter(
            stack_layers(per_layer, 11).astype(jnp.bfloat16), "ctx", scatter_dimension=1, tiled=True
        ).astype(jnp.float32),
    )
    totals = (
        lax.all_gather(shares[0].astype(jnp.bfloat16), "ctx", axis=1, tiled=True).astype(
            jnp.float32
        ),
        lax.all_gather(shares[1].astype(jnp.bfloat16), "ctx", axis=1, tiled=True).astype(
            jnp.float32
        ),
        lax.all_gather(shares[2].astype(jnp.bfloat16), "ctx", axis=1, tiled=True).astype(
            jnp.float32
        ),
        lax.all_gather(shares[3].astype(jnp.bfloat16), "ctx", axis=1, tiled=True).astype(
            jnp.float32
        ),
        lax.all_gather(shares[4].astype(jnp.bfloat16), "ctx", axis=1, tiled=True).astype(
            jnp.float32
        ),
        lax.all_gather(shares[5].astype(jnp.bfloat16), "ctx", axis=2, tiled=True).astype(
            jnp.float32
        ),
        lax.all_gather(shares[6].astype(jnp.bfloat16), "ctx", axis=2, tiled=True).astype(
            jnp.float32
        ),
        lax.all_gather(shares[7].astype(jnp.bfloat16), "ctx", axis=1, tiled=True).astype(
            jnp.float32
        ),
        lax.all_gather(shares[8].astype(jnp.bfloat16), "ctx", axis=1, tiled=True).astype(
            jnp.float32
        ),
        lax.all_gather(shares[9].astype(jnp.bfloat16), "ctx", axis=1, tiled=True).astype(
            jnp.float32
        ),
        lax.all_gather(shares[10].astype(jnp.bfloat16), "ctx", axis=2, tiled=True).astype(
            jnp.float32
        ),
        lax.all_gather(shares[11].astype(jnp.bfloat16), "ctx", axis=1, tiled=True).astype(
            jnp.float32
        ),
    )
    return (
        output,
        grad,
        totals[0],
        totals[1],
        totals[2],
        totals[3],
        totals[4],
        totals[5],
        totals[6],
        totals[7],
        totals[8],
        totals[9],
        totals[10],
        totals[11],
    )


def solution(mesh):
    in_specs = (
        P(None, "ctx", None),
        P(),
        P(),
        P(),
        P(),
        P(None, None, None, "tp"),
        P(None, None, "tp"),
        P(None, "tp", None),
        P(),
        P(None, None, "tp"),
        P(None, "tp"),
        P(None, "tp", None),
        P(),
        P(None, "ctx", None),
    )
    out_specs = (
        P(None, "ctx", None),
        P(None, "ctx", None),
        P(),
        P(),
        P(),
        P(),
        P(None, None, None, "tp"),
        P(None, None, "tp"),
        P(None, "tp", None),
        P(),
        P(None, None, "tp"),
        P(None, "tp"),
        P(None, "tp", None),
        P(),
    )
    return jax.shard_map(
        on_device, mesh=mesh, in_specs=in_specs, out_specs=out_specs, check_vma=False
    )
```

profile of v0, /device:TPU:0, one launch (start us, length us, event | category | flops | bytes accessed | tf_op | source)
XLA Modules:
  0.0 2396.0 jit_solution(4642939205093169725)
XLA Ops:
  21.8 78.2 %all-gather.12.cloned.1.call-done = bf16[1,4096,384]{1,2,0:T(8,128)(2,1)} async-done(((bf16[1,128,384]{1,2,0:T(8,128)(2,1)}), bf16[1,4096,384]{1,2,0:T(8,128)(2,1)}) %all-gather.12.cloned.1.call-update) | async-done | bytes 3145744 | tf_op jit(solution)/shard_map/all_gather | solution.py:59
  114.4 33.2 %all-reduce.19.cloned.1.call-done = bf16[1,128,768]{2,1,0:T(8,128)(2,1)} async-done(((bf16[1,128,768]{2,1,0:T(8,128)(2,1)}), bf16[1,128,768]{2,1,0:T(8,128)(2,1)}) %all-reduce.19.cloned.1.call-update) | async-done | bytes 196624 | tf_op jit(solution)/shard_map/psum | solution.py:250
  152.6 83.1 %all-gather.14.cloned.1.call-done = bf16[1,4096,384]{1,2,0:T(8,128)(2,1)} async-done(((bf16[1,128,384]{1,2,0:T(8,128)(2,1)}), bf16[1,4096,384]{1,2,0:T(8,128)(2,1)}) %all-gather.14.cloned.1.call-update) | async-done | bytes 3145744 | tf_op jit(solution)/shard_map/all_gather | solution.py:59
  247.0 17.1 conditional.9
  264.2 11.0 copy.77
  286.9 15.0 conditional.8
  301.9 201.1 %reduce-scatter.17.cloned.1.call-done = bf16[128,384]{1,0:T(8,128)(2,1)} async-done(((bf16[4096,384]{1,0:T(8,128)(2,1)}), bf16[128,384]{1,0:T(8,128)(2,1)}) %reduce-scatter.17.cloned.1.call-update) | async-done | bytes 98320
  509.3 34.0 %all-reduce.25.cloned.1.call-done = (bf16[1,128,768]{2,1,0:T(8,128)(2,1)}, bf16[1,128,768]{2,1,0:T(8,128)(2,1)}) async-done(((bf16[1,128,768]{2,1,0:T(8,128)(2,1)}, bf16[1,128,768]{2,1,0:T(8,128)(2,1)}), (bf16[1,128,768]{2,1,0:T(8,128)(2,1)}, bf16[1,128,768]{2,1,0:T(8,128)(2,1)})) %all-reduce.25.cloned.1.call-update) | async-done | bytes 393232 | tf_op jit(solution)/shard_map/psum | solution.py:343
  552.8 19.5 conditional.11
  572.3 14.5 copy.79
  610.4 12.6 conditional.10
  635.3 182.5 %reduce-scatter.19.cloned.1.call-done = bf16[128,384]{1,0:T(8,128)(2,1)} async-done(((bf16[4096,384]{1,0:T(8,128)(2,1)}), bf16[128,384]{1,0:T(8,128)(2,1)}) %reduce-scatter.19.cloned.1.call-update) | async-done | bytes 98320
  832.6 213.2 %reduce-scatter.21.cloned.1.call-done = bf16[24,1536]{1,0:T(8,128)(2,1)} async-done(((bf16[768,1536]{1,0:T(8,128)(2,1)}), bf16[24,1536]{1,0:T(8,128)(2,1)}) %reduce-scatter.21.cloned.1.call-update) | async-done | bytes 73744
  1048.7 370.2 %all-reduce.21.cloned.1.call-done = (bf16[2,768,3,192]{3,0,2,1:T(2,128)(2,1)}, bf16[2,192,768]{1,0,2:T(2,128)(2,1)}, bf16[2,768,768]{1,0,2:T(2,128)(2,1)}) async-done(((bf16[2,768,3,192]{3,0,2,1:T(2,128)(2,1)}, bf16[2,192,768]{1,0,2:T(2,128)(2,1)}, bf16[2,768,768]{1,0,2:T(2,128)(2,1)}), (bf16[2,768,3,192]{3,0,2,1:T(2,128)(2,1)}, bf16[2,192,768]{1,0,2:T(2,128)(2,1)}, ...) | async-done | bytes 4718608
  1423.5 38.1 %all-reduce.23.cloned.1.call-done = (bf16[1,128,768]{2,1,0:T(8,128)(2,1)}, bf16[1,128,768]{2,1,0:T(8,128)(2,1)}, bf16[1,128,768]{2,1,0:T(8,128)(2,1)}) async-done(((bf16[1,128,768]{2,1,0:T(8,128)(2,1)}, bf16[1,128,768]{2,1,0:T(8,128)(2,1)}, bf16[1,128,768]{2,1,0:T(8,128)(2,1)}), (bf16[1,128,768]{2,1,0:T(8,128)(2,1)}, bf16[1,128,768]{2,1,0:T(8,128)(2,1)}, ...) | async-done | bytes 589840 | tf_op jit(solution)/shard_map/psum | solution.py:343
  1466.6 184.0 %all-reduce.10 = (bf16[2,3,192]{2,1,0:T(4,128)(2,1)S(1)}, bf16[2,768]{1,0:T(2,128)(2,1)S(1)}, bf16[2,768]{1,0:T(2,128)(2,1)S(1)}, bf16[2,768]{1,0:T(2,128)(2,1)S...) all-reduce(bf16[2,3,192]{2,1,0:T(4,128)(2,1)S(1)} %pad_maximum_fusi, ...), channel_id=9, replica_groups=mesh['ctx'=32,'tp'=4] {'ctx'}, use_global_device_ids=true, to_apply=%region_53.54.clone | all-reduce | flops 10368 | bytes 41472
  1650.8 88.0 %all_gather.51 = bf16[2,3,192]{1,0,2:T(2,128)(2,1)S(1)} all-gather(bf16[2,3,6]{1,0,2:T(2,128)(2,1)S(1)} %copy.66), channel_id=1, replica_groups=mesh['ctx'=32,'tp'=4] {'ctx'}, dimensions={2}, use_global_device_ids=true | all-gather | bytes 2376 | tf_op jit(solution)/shard_map/all_gather | solution.py:418
  1739.6 89.0 %all-gather.4 = bf16[32,24,2]{1,2,0:T(2,128)(2,1)S(1)} all-gather(bf16[1,24,2]{1,2,0:T(2,128)(2,1)S(1)} %fusion.198), channel_id=1, replica_groups=mesh['ctx'=32,'tp'=4] {'ctx'}, dimensions={0}, use_global_device_ids=true | all-gather | bytes 3168 | tf_op jit(solution)/shard_map/all_gather | solution.py:424
  1828.9 86.9 %all-gather = bf16[32,24,2]{1,2,0:T(2,128)(2,1)S(1)} all-gather(bf16[1,24,2]{1,2,0:T(2,128)(2,1)S(1)} %fusion.194), channel_id=1, replica_groups=mesh['ctx'=32,'tp'=4] {'ctx'}, dimensions={0}, use_global_device_ids=true | all-gather | bytes 3168 | tf_op jit(solution)/shard_map/all_gather | solution.py:403
  1916.7 88.9 %all-gather.1 = bf16[32,24,2]{1,2,0:T(2,128)(2,1)S(1)} all-gather(bf16[1,24,2]{1,2,0:T(2,128)(2,1)S(1)} %fusion.195), channel_id=1, replica_groups=mesh['ctx'=32,'tp'=4] {'ctx'}, dimensions={0}, use_global_device_ids=true | all-gather | bytes 3168 | tf_op jit(solution)/shard_map/all_gather | solution.py:406
  2006.6 86.9 %all-gather.2 = bf16[32,24,2]{1,2,0:T(2,128)(2,1)S(1)} all-gather(bf16[1,24,2]{1,2,0:T(2,128)(2,1)S(1)} %fusion.196), channel_id=1, replica_groups=mesh['ctx'=32,'tp'=4] {'ctx'}, dimensions={0}, use_global_device_ids=true | all-gather | bytes 3168 | tf_op jit(solution)/shard_map/all_gather | solution.py:409
  2094.4 88.9 %all-gather.3 = bf16[32,24,2]{1,2,0:T(2,128)(2,1)S(1)} all-gather(bf16[1,24,2]{1,2,0:T(2,128)(2,1)S(1)} %fusion.197), channel_id=1, replica_groups=mesh['ctx'=32,'tp'=4] {'ctx'}, dimensions={0}, use_global_device_ids=true | all-gather | bytes 3168 | tf_op jit(solution)/shard_map/all_gather | solution.py:412
  2184.2 86.9 %all-gather.5 = bf16[32,24,2]{1,2,0:T(2,128)(2,1)S(1)} all-gather(bf16[1,24,2]{1,2,0:T(2,128)(2,1)S(1)} %fusion.199), channel_id=1, replica_groups=mesh['ctx'=32,'tp'=4] {'ctx'}, dimensions={0}, use_global_device_ids=true | all-gather | bytes 3168 | tf_op jit(solution)/shard_map/all_gather | solution.py:430
  2278.1 93.5 %all_gather.52 = bf16[2,192,768]{1,0,2:T(2,128)(2,1)S(1)} all-gather(bf16[2,192,24]{1,0,2:T(2,128)(2,1)S(1)} %constant_dynamic-slice_fusion.3), channel_id=1, replica_groups=mesh['ctx'=32,'tp'=4] {'ctx'}, dimensions={2}, use_global_device_ids=true | all-gather | bytes 608256 | tf_op jit(solution)/shard_map/all_gather | solution.py:421
  (472 shorter events, 244.4 us)
Async XLA Ops:
  7.2 92.8 %all-gather.12.cloned.1.call-start = ((), (), s32[]{:S(2)}) async-start(), calls=%async_computation.3 | async-start | bytes 3244032 | tf_op jit(solution)/shard_map/all_gather | solution.py:59
  15.0 132.5 %all-reduce.19.cloned.1.call-start = ((), (), s32[]{:S(2)}) async-start(), calls=%async_computation.4 | async-start | bytes 393216 | tf_op jit(solution)/shard_map/psum | solution.py:250
  113.7 122.0 %all-gather.14.cloned.1.call-start = ((), (), s32[]{:S(2)}) async-start(), calls=%async_computation.5 | async-start | bytes 3244032 | tf_op jit(solution)/shard_map/all_gather | solution.py:59
  152.2 350.8 %reduce-scatter.17.cloned.1.call-start = ((), (), s32[]{:S(2)}) async-start(), calls=%async_computation.9 | async-start | bytes 3244032
  280.2 263.2 %all-reduce.25.cloned.1.call-start = ((), (), s32[]{:S(2)}) async-start(), calls=%async_computation.14 | async-start | bytes 786432 | tf_op jit(solution)/shard_map/psum | solution.py:343
  509.3 308.5 %reduce-scatter.19.cloned.1.call-start = ((), (), s32[]{:S(2)}) async-start(), calls=%async_computation.10 | async-start | bytes 3244032
  591.7 454.1 %reduce-scatter.21.cloned.1.call-start = ((), (), s32[]{:S(2)}) async-start(), calls=%async_computation.11 | async-start | bytes 2433024
  602.4 816.5 %all-reduce.21.cloned.1.call-start = ((), (), s32[]{:S(2)}) async-start(), calls=%async_computation.12 | async-start | bytes 11010048
  825.6 636.1 %all-reduce.23.cloned.1.call-start = ((), (), s32[]{:S(2)}) async-start(), calls=%async_computation.13 | async-start | bytes 1179648 | tf_op jit(solution)/shard_map/psum | solution.py:343
  828.8 594.5 %copy-start.111 = (bf16[768]{0:T(1024)(128)(2,1)S(1)}, bf16[768]{0:T(1024)(128)(2,1)}, u32[]{:S(2)}) copy-start(bf16[768]{0:T(1024)(128)(2,1)} %get-tuple-element.372) | copy-start | bytes 4612
  828.8 594.5 %copy-start.100 = (bf16[768]{0:T(1024)(128)(2,1)S(1)}, bf16[768]{0:T(1024)(128)(2,1)}, u32[]{:S(2)}) copy-start(bf16[768]{0:T(1024)(128)(2,1)} %get-tuple-element.299) | copy-start | bytes 4612
  828.8 594.5 %copy-start.51 = (bf16[1,128,1,192]{1,3,2,0:T(8,128)(2,1)S(1)}, bf16[1,128,1,192]{1,3,2,0:T(8,128)(2,1)}, u32[]{:S(2)}) copy-start(bf16[1,128,1,192]{1,3,2,0:T(8,128)(2,1)} %get-tuple-element.331) | copy-start | bytes 147460
  831.5 632.2 %copy-start.74 = (f32[128]{0:T(128)S(1)}, f32[128]{0:T(128)}, u32[]{:S(2)}) copy-start(f32[128]{0:T(128)} %copy-done.71) | copy-start | bytes 1540
  831.5 633.4 %copy-start.108 = (f32[128]{0:T(128)S(1)}, f32[128]{0:T(128)}, u32[]{:S(2)}) copy-start(f32[128]{0:T(128)} %copy-done.107) | copy-start | bytes 1540
  831.5 633.5 %copy-start.89 = (f32[128]{0:T(128)S(1)}, f32[128]{0:T(128)}, u32[]{:S(2)}) copy-start(f32[128]{0:T(128)} %copy-done.86) | copy-start | bytes 1540
  832.5 1439.4 %copy-start.9 = (f32[1,128,768]{2,1,0:T(8,128)S(1)}, f32[1,128,768]{2,1,0:T(8,128)}, u32[]{:S(2)}) copy-start(f32[1,128,768]{2,1,0:T(8,128)} %copy-done.8) | copy-start | bytes 1179652
  832.6 1439.4 %copy-start.79 = (f32[768]{0:T(1024)S(1)}, f32[768]{0:T(1024)}, u32[]{:S(2)}) copy-start(f32[768]{0:T(1024)} %get-tuple-element.272) | copy-start | bytes 9220
  832.6 1439.4 %copy-start.80 = (f32[768]{0:T(1024)S(1)}, f32[768]{0:T(1024)}, u32[]{:S(2)}) copy-start(f32[768]{0:T(1024)} %get-tuple-element.379) | copy-start | bytes 9220
  832.6 1440.6 %all-gather.18.cloned.1.call-start = ((), (), s32[]{:S(2)}) async-start(), calls=%async_computation.7 | async-start | bytes 2433024 | tf_op jit(solution)/shard_map/all_gather | solution.py:427
  1047.4 1326.1 %all-gather.16.cloned.1.call-start = ((), (), s32[]{:S(2)}) async-start(), calls=%async_computation.6 | async-start | bytes 2433024 | tf_op jit(solution)/shard_map/all_gather | solution.py:415
  1420.5 960.1 %all-gather.20.cloned.1.call-start = ((), (), s32[]{:S(2)}) async-start(), calls=%async_computation.8 | async-start | bytes 2433024 | tf_op jit(solution)/shard_map/all_gather | solution.py:433
  1461.6 810.3 %copy-start.15 = (bf16[1,128,768]{2,1,0:T(8,128)(2,1)S(1)}, bf16[1,128,768]{2,1,0:T(8,128)(2,1)}, u32[]{:S(2)}) copy-start(bf16[1,128,768]{2,1,0:T(8,128)(2,1)} %get-tuple-element.294) | copy-start | bytes 589828
  1461.6 810.4 %copy-start.16 = (bf16[1,128,768]{2,1,0:T(8,128)(2,1)S(1)}, bf16[1,128,768]{2,1,0:T(8,128)(2,1)}, u32[]{:S(2)}) copy-start(bf16[1,128,768]{2,1,0:T(8,128)(2,1)} %get-tuple-element.295) | copy-start | bytes 589828
  1461.6 810.4 %copy-start.47 = (bf16[1,128,768]{2,1,0:T(8,128)(2,1)S(1)}, bf16[1,128,768]{2,1,0:T(8,128)(2,1)}, u32[]{:S(2)}) copy-start(bf16[1,128,768]{2,1,0:T(8,128)(2,1)} %get-tuple-element.296) | copy-start | bytes 589828
  (102 other events, 8567.6 us)
Sparse Core Ops, SparseCore 0:
  15.1 84.8 all-gather.11
  113.8 33.7 all-reduce.18
  152.3 83.3 all-gather.13
  280.3 222.6 reduce-scatter.16
  509.4 33.9 all-reduce.24
  591.8 225.9 reduce-scatter.18
  823.3 222.4 reduce-scatter.20
  1049.9 368.9 all-reduce.20
  1422.8 38.8 all-reduce.22
  1465.1 72.8 all-gather.17
  1541.6 70.3 all-gather.15
  1615.5 70.3 all-gather.19
where the time goes:
time: 2410 us; the launch traced here: 2400 us
  waiting for transfers between devices  1230 us (51%)
  blocking collectives  893 us (37%)
  local copies, waits for them, and re-layouts  107 us (4%)
  matrix products  88.5 us (4%)
  other arithmetic  53.8 us (2%)
    unnamed x16, waiting for transfers between devices  967 us
    unnamed x1, blocking collectives  184 us
    all_gather x2, waiting for transfers between devices, forward_attention(): piece = lax.all_gather(key_value, 'ctx', axis=1, tiled=True)  161 us
    all_gather x1, blocking collectives, on_device(): lax.all_gather(shares[6].astype(jnp.bfloat16), 'ctx', axis=2, tiled=True)  93.5 us
    all_gather x1, blocking collectives, on_device(): lax.all_gather(shares[7].astype(jnp.bfloat16), 'ctx', axis=1, tiled=True)  89 us
    all_gather x1, blocking collectives, on_device(): lax.all_gather(shares[3].astype(jnp.bfloat16), 'ctx', axis=1, tiled=True)  88.9 us
    all_gather x1, blocking collectives, on_device(): lax.all_gather(shares[1].astype(jnp.bfloat16), 'ctx', axis=1, tiled=True)  88.9 us
    all_gather x1, blocking collectives, on_device(): lax.all_gather(shares[5].astype(jnp.bfloat16), 'ctx', axis=2, tiled=True)  88 us
  transfers between devices with their start and end apart: 12, of which 9 were waited for; matrix products, arithmetic and copies ran while one was open for 5% of the time, Pallas kernels for 0%

commit v1 on v0

v1 whole, which is shorter than its diff:
```python
import functools
import math

import jax
import jax.numpy as jnp
from jax import lax
from jax.experimental import pallas as pl
from jax.experimental.pallas import tpu as pltpu
from jax.sharding import PartitionSpec as P

HD = 64
ROT = 16
LAYERS = 2
NORM_EPSILON = 1e-05
MASKED = -1e30
F32 = jnp.float32
BF16 = jnp.bfloat16
ROWS = 128
D = 768
HEADS = 3
CTX = 32
TP = 4
CHUNK = 512
PER = CHUNK // ROWS
QUARTER = ROWS // TP
SCALE = HD**-0.5
G1, S1, G2, S2, BUP, BOUT, BQKV = range(7)
QKV_ROWS, OUT_ROWS, UP_ROWS, DOWN_ROWS = 576, 192, 768, 768
GRAD_ROWS = QKV_ROWS + OUT_ROWS + UP_ROWS + DOWN_ROWS

NN = (((1,), (0,)), ((), ()))
NT = (((1,), (1,)), ((), ()))
TN = (((0,), (0,)), ((), ()))


def dot(a, b, dims=NN):
    return lax.dot_general(a, b, dims, preferred_element_type=F32)


def remote(src, dst, send, recv, ctx=None, tp=None):
    where = {}
    if ctx is not None:
        where["ctx"] = ctx
    if tp is not None:
        where["tp"] = tp
    return pltpu.make_async_remote_copy(
        src_ref=src,
        dst_ref=dst,
        send_sem=send,
        recv_sem=recv,
        device_id=where,
        device_id_type=pl.DeviceIdType.MESH,
    )


def greet(ctx_peers, tp_peers):
    barrier = pltpu.get_barrier_semaphore()
    for peer in ctx_peers:
        pl.semaphore_signal(
            barrier, inc=1, device_id={"ctx": peer}, device_id_type=pl.DeviceIdType.MESH
        )
    for peer in tp_peers:
        pl.semaphore_signal(
            barrier, inc=1, device_id={"tp": peer}, device_id_type=pl.DeviceIdType.MESH
        )
    return barrier, len(ctx_peers) + len(tp_peers)


def greet_all(me, my_tp):
    barrier = pltpu.get_barrier_semaphore()

    @pl.loop(1, CTX)
    def _(step):
        pl.semaphore_signal(
            barrier,
            inc=1,
            device_id={"ctx": lax.rem(me + step, CTX)},
            device_id_type=pl.DeviceIdType.MESH,
        )

    for step in range(1, TP):
        pl.semaphore_signal(
            barrier,
            inc=1,
            device_id={"tp": lax.rem(my_tp + step, TP)},
            device_id_type=pl.DeviceIdType.MESH,
        )
    return barrier


def centre(residual):
    mean_value = jnp.mean(residual, axis=-1, keepdims=True)
    centred = residual - mean_value
    variance = jnp.mean(centred * centred, axis=-1, keepdims=True)
    inverse = lax.rsqrt(variance + NORM_EPSILON)
    return centred * inverse, inverse


def turn(values, rot_ref, sign):
    width = values.shape[1]
    count = width // 128
    cosine = jnp.concatenate([rot_ref[0]] * count, axis=1)
    after = jnp.concatenate([rot_ref[1]] * count, axis=1)
    before = jnp.concatenate([rot_ref[2]] * count, axis=1)
    turned = pltpu.roll(values, 8, 1) * after + pltpu.roll(values, width - 8, 1) * before
    return values * cosine + sign * turned


def tp_sum(part, my_tp, buffers, sems):
    mine, out, slots, gathered = buffers
    send, recv = sems
    mine[...] = part
    out[...] = part.astype(BF16)
    own = pl.ds(pl.multiple_of(my_tp * QUARTER, QUARTER), QUARTER)
    copies = []
    for step in range(1, TP):
        peer = lax.rem(my_tp + step, TP)
        rows = pl.ds(pl.multiple_of(peer * QUARTER, QUARTER), QUARTER)
        copy = remote(
            out.at[rows], slots.at[step - 1], send.at[step - 1], recv.at[step - 1], tp=peer
        )
        copy.start()
        copies.append(copy)
    total = mine[own, :]
    for step in range(1, TP):
        copies[step - 1].wait_recv()
        total = total + slots[step - 1].astype(F32)
    gathered[own, :] = total.astype(BF16)
    for step in range(1, TP):
        peer = lax.rem(my_tp + step, TP)
        copy = remote(
            gathered.at[own],
            gathered.at[own],
            send.at[TP - 2 + step],
            recv.at[TP - 2 + step],
            tp=peer,
        )
        copy.start()
        copies.append(copy)
    for step in range(1, TP):
        source = lax.rem(my_tp + TP - step, TP)
        rows = pl.ds(pl.multiple_of(source * QUARTER, QUARTER), QUARTER)
        remote(
            gathered.at[rows],
            gathered.at[rows],
            send.at[TP - 2 + step],
            recv.at[TP - 2 + step],
            tp=source,
        ).wait_recv()
    for copy in copies:
        copy.wait_send()
    return gathered[...].astype(F32)


TP_BUFFERS = [
    pltpu.VMEM((ROWS, D), F32),
    pltpu.VMEM((ROWS, D), BF16),
    pltpu.VMEM((TP - 1, QUARTER, D), BF16),
    pltpu.VMEM((ROWS, D), BF16),
]
TP_SEMS = [pltpu.SemaphoreType.DMA((2 * TP - 2,)), pltpu.SemaphoreType.DMA((2 * TP - 2,))]


def forward_kernel(
    layer,
    resid_ref,
    vec_ref,
    rot_ref,
    wq_hbm,
    wo_hbm,
    wu_hbm,
    wd_hbm,
    next_ref,
    kv_ref,
    qp_ref,
    att_ref,
    lse_ref,
    pre_ref,
    hid_ref,
    wq,
    wo,
    wu,
    wd,
    acc,
    top,
    load_sem,
    kv_send,
    kv_recv,
    tp_mine,
    tp_out,
    tp_slots,
    tp_gathered,
    tp_send,
    tp_recv,
):
    me = lax.axis_index("ctx")
    my_tp = lax.axis_index("tp")
    loads = []
    for index, (src, dst) in enumerate(((wq_hbm, wq), (wu_hbm, wu), (wd_hbm, wd), (wo_hbm, wo))):
        load = pltpu.make_async_copy(src.at[layer], dst, load_sem.at[index])
        load.start()
        loads.append(load)
    barrier = greet_all(me, my_tp)

    residual = resid_ref[...]
    vec = vec_ref.at[layer]
    hat, _ = centre(residual)
    normed = (hat * vec[G1 : G1 + 1, :] + vec[S1 : S1 + 1, :]).astype(BF16)
    loads[0].wait()
    merged = dot(normed, wq[...]) + vec[BQKV : BQKV + 1, :]
    merged = turn(merged, rot_ref, 1.0).astype(BF16)
    own = pl.ds(pl.multiple_of(me * ROWS, ROWS), ROWS)
    kv_ref[own, :] = merged[:, :384]
    qp_ref[...] = merged[:, 384:]
    pl.semaphore_wait(barrier, CTX - 1 + TP - 1)

    @pl.loop(me + 1, CTX)
    def _(target):
        remote(
            kv_ref.at[own], kv_ref.at[own], kv_send.at[target], kv_recv.at[me], ctx=target
        ).start()

    @pl.loop(me + 1, (me // PER + 1) * PER)
    def _(block):
        kv_ref[pl.ds(pl.multiple_of(block * ROWS, ROWS), ROWS), :] = jnp.zeros((ROWS, 384), BF16)

    normed = (hat * vec[G2 : G2 + 1, :] + vec[S2 : S2 + 1, :]).astype(BF16)
    loads[1].wait()
    pre = dot(normed, wu[...]) + vec[BUP : BUP + 1, :]
    pre_ref[...] = pre
    hidden = (pre * (1.0 + lax.erf(pre * math.sqrt(0.5))) * 0.5).astype(BF16)
    hid_ref[...] = hidden
    loads[2].wait()
    branch = dot(hidden, wd[...])
    next_ref[...] = branch

    acc[...] = jnp.zeros_like(acc)
    top[...] = jnp.zeros_like(top)
    for head in range(HEADS):
        top[head : head + 1, :] = jnp.full((1, ROWS), MASKED, F32)

    @pl.loop(0, me // PER + 1)
    def _(chunk):
        @pl.loop(chunk * PER, jnp.minimum(chunk * PER + PER, me))
        def _(source):
            rows = pl.ds(pl.multiple_of(source * ROWS, ROWS), ROWS)
            remote(
                kv_ref.at[rows], kv_ref.at[rows], kv_send.at[source], kv_recv.at[source], ctx=source
            ).wait_recv()

        keys = pl.ds(pl.multiple_of(chunk * CHUNK, CHUNK), CHUNK)
        key_pos = chunk * CHUNK + lax.broadcasted_iota(jnp.int32, (CHUNK, ROWS), 0)
        query_pos = me * ROWS + lax.broadcasted_iota(jnp.int32, (CHUNK, ROWS), 1)
        allowed = key_pos <= query_pos
        for head in range(HEADS):
            lanes = slice(128 * head, 128 * head + 128)
            block = kv_ref[keys, lanes]
            scores = dot(block, qp_ref[:, lanes], NT) * SCALE
            scores = jnp.where(allowed, scores, MASKED)
            old = top[head : head + 1, :]
            new = jnp.maximum(old, jnp.max(scores, axis=0, keepdims=True))
            weights = jnp.exp(scores - new)
            shrink = jnp.exp(old - new)
            top[head : head + 1, :] = new
            top[4 + head : 5 + head, :] = top[4 + head : 5 + head, :] * shrink + jnp.sum(
                weights, axis=0, keepdims=True
            )
            acc[head] = acc[head] * shrink + dot(block, weights.astype(BF16), TN)

    for head in range(HEADS):
        total = top[4 + head : 5 + head, :]
        att_ref[64 * head : 64 * head + 64, :] = acc[head, 64:, :] / total
        lse_ref[head : head + 1, :] = top[head : head + 1, :] + jnp.log(total)
    lse_ref[HEADS:, :] = jnp.zeros((8 - HEADS, ROWS), F32)
    loads[3].wait()
    branch = next_ref[...] + dot(att_ref[...].astype(BF16), wo[...], TN)
    branch = tp_sum(
        branch, my_tp, (tp_mine, tp_out, tp_slots, tp_gathered), (tp_send, tp_recv)
    )
    next_ref[...] = resid_ref[...] + branch + vec[BOUT : BOUT + 1, :]

    @pl.loop(me + 1, CTX)
    def _(target):
        remote(
            kv_ref.at[own], kv_ref.at[own], kv_send.at[target], kv_recv.at[me], ctx=target
        ).wait_send()


def vmem(count):
    return [pl.BlockSpec(memory_space=pltpu.VMEM)] * count


def hbm(count):
    return [pl.BlockSpec(memory_space=pl.ANY)] * count


def forward(layer, residual, vec, rot, wq, wo, wu, wd):
    return pl.pallas_call(
        functools.partial(forward_kernel, layer),
        name=f"layer_forward_{layer}",
        out_shape=[
            jax.ShapeDtypeStruct((ROWS, D), F32),
            jax.ShapeDtypeStruct((CTX * ROWS, 384), BF16),
            jax.ShapeDtypeStruct((ROWS, 384), BF16),
            jax.ShapeDtypeStruct((192, ROWS), F32),
            jax.ShapeDtypeStruct((8, ROWS), F32),
            jax.ShapeDtypeStruct((ROWS, D), F32),
            jax.ShapeDtypeStruct((ROWS, D), BF16),
        ],
        in_specs=vmem(3) + hbm(4),
        out_specs=vmem(7),
        scratch_shapes=[
            pltpu.VMEM((D, D), BF16),
            pltpu.VMEM((192, D), BF16),
            pltpu.VMEM((D, D), BF16),
            pltpu.VMEM((D, D), BF16),
            pltpu.VMEM((HEADS, 128, ROWS), F32),
            pltpu.VMEM((8, ROWS), F32),
            pltpu.SemaphoreType.DMA((4,)),
            pltpu.SemaphoreType.DMA((CTX,)),
            pltpu.SemaphoreType.DMA((CTX,)),
            *TP_BUFFERS,
            *TP_SEMS,
        ],
        compiler_params=pltpu.CompilerParams(
            collective_id=layer, has_side_effects=True, vmem_limit_bytes=48 << 20
        ),
    )(residual, vec, rot, wq, wo, wu, wd)


def backward_kernel(
    layer,
    grad_ref,
    resid_ref,
    vec_ref,
    rot_ref,
    kv_ref,
    qp_ref,
    att_ref,
    lse_ref,
    pre_ref,
    hid_ref,
    wq_hbm,
    wp_hbm,
    wu_hbm,
    wd_hbm,
    out_ref,
    weight_ref,
    small_ref,
    wq,
    wp,
    wu,
    wd,
    terms,
    slots,
    left,
    right,
    query,
    delta,
    norm_part,
    load_sem,
    kv_send,
    kv_recv,
    tp_mine,
    tp_out,
    tp_slots,
    tp_gathered,
    tp_send,
    tp_recv,
):
    me = lax.axis_index("ctx")
    my_tp = lax.axis_index("tp")
    loads = []
    for index, (src, dst) in enumerate(((wp_hbm, wp), (wd_hbm, wd), (wu_hbm, wu), (wq_hbm, wq))):
        load = pltpu.make_async_copy(src.at[layer], dst, load_sem.at[index])
        load.start()
        loads.append(load)
    barrier = greet_all(me, my_tp)
    vec = vec_ref.at[layer]

    low = grad_ref[...].astype(BF16)
    loads[0].wait()
    mixed = dot(low, wp[...], NT).astype(BF16)
    turned = dot(wp[...], low, NT).astype(BF16).astype(F32)
    for head in range(HEADS):
        lanes = slice(128 * head, 128 * head + 128)
        left[head, :ROWS, :] = qp_ref[:, lanes]
        left[head, ROWS:, :] = mixed[:, lanes]
        right[head, :ROWS, :] = (qp_ref[:, lanes].astype(F32) * SCALE).astype(BF16)
        right[head, ROWS:, :] = mixed[:, lanes]
        delta[head : head + 1, :] = jnp.sum(
            turned[128 * head + 64 : 128 * head + 128, :] * att_ref[64 * head : 64 * head + 64, :],
            axis=0,
            keepdims=True,
        )
    query[...] = jnp.zeros_like(query)
    pl.semaphore_wait(barrier, CTX - 1 + TP - 1)

    def term_copy(target):
        rows = pl.ds(pl.multiple_of(target * ROWS, ROWS), ROWS)
        return remote(
            terms.at[rows], slots.at[me], kv_send.at[target], kv_recv.at[me], ctx=target
        )

    @pl.loop(0, me // PER + 1)
    def _(chunk):
        keys = pl.ds(pl.multiple_of(chunk * CHUNK, CHUNK), CHUNK)
        key_pos = chunk * CHUNK + lax.broadcasted_iota(jnp.int32, (CHUNK, ROWS), 0)
        query_pos = me * ROWS + lax.broadcasted_iota(jnp.int32, (CHUNK, ROWS), 1)
        allowed = key_pos <= query_pos
        for head in range(HEADS):
            lanes = slice(128 * head, 128 * head + 128)
            block = kv_ref[keys, lanes]
            both = dot(block, left[head], NT)
            probs = jnp.where(
                allowed, jnp.exp(both[:, :ROWS] * SCALE - lse_ref[head : head + 1, :]), 0.0
            )
            scores = (probs * (both[:, ROWS:] - delta[head : head + 1, :])).astype(BF16)
            terms[keys, lanes] = dot(
                jnp.concatenate([scores, probs.astype(BF16)], axis=1), right[head]
            ).astype(BF16)
            query[head] += dot(scores, block, TN)

        @pl.loop(chunk * PER, jnp.minimum(chunk * PER + PER, me))
        def _(target):
            term_copy(target).start()

    small_ref[...] = jnp.zeros_like(small_ref)
    small_ref[4:5, :] = jnp.sum(grad_ref[...], axis=0, keepdims=True)
    weight_ref[QKV_ROWS : QKV_ROWS + OUT_ROWS, :] = dot(att_ref[...].astype(BF16), low).astype(BF16)
    weight_ref[QKV_ROWS + OUT_ROWS + UP_ROWS :, :] = dot(hid_ref[...], low, TN).astype(BF16)
    loads[1].wait()
    hidden_grad = dot(low, wd[...], NT)
    pre = pre_ref[...]
    slope = 0.5 * (1.0 + lax.erf(pre * math.sqrt(0.5))) + pre * jnp.exp(
        -0.5 * pre * pre
    ) * (1.0 / math.sqrt(2.0 * math.pi))
    pre_grad = (hidden_grad * slope).astype(BF16)
    small_ref[6:7, :] = jnp.sum(pre_grad.astype(F32), axis=0, keepdims=True)
    hat, inverse = centre(resid_ref[...])
    gain_one, gain_two = vec[G1 : G1 + 1, :], vec[G2 : G2 + 1, :]
    normed_two = (hat * gain_two + vec[S2 : S2 + 1, :]).astype(BF16)
    weight_ref[QKV_ROWS + OUT_ROWS : QKV_ROWS + OUT_ROWS + UP_ROWS, :] = dot(
        normed_two, pre_grad, TN
    ).astype(BF16)
    loads[2].wait()
    grad_two = dot(pre_grad, wu[...], NT)
    small_ref[2:3, :] = jnp.sum(grad_two * hat, axis=0, keepdims=True)
    small_ref[3:4, :] = jnp.sum(grad_two, axis=0, keepdims=True)
    norm_part[...] = grad_two * gain_two

    own = pl.ds(pl.multiple_of(me * ROWS, ROWS), ROWS)
    out_ref[:, :384] = terms[own, :].astype(F32)

    @pl.loop(me + 1, CTX)
    def _(source):
        remote(
            terms.at[own], slots.at[source], kv_send.at[source], kv_recv.at[source], ctx=source
        ).wait_recv()
        out_ref[:, :384] += slots[source].astype(F32)

    lane = lax.broadcasted_iota(jnp.int32, (ROWS, 128), 1)
    for head in range(HEADS):
        out_ref[:, 384 + 128 * head : 512 + 128 * head] = jnp.where(
            lane < HD, query[head] * SCALE, 0.0
        )
    merged = turn(out_ref[...], rot_ref, -1.0).astype(BF16)
    hat, inverse = centre(resid_ref[...])
    normed_one = (hat * gain_one + vec[S1 : S1 + 1, :]).astype(BF16)
    weight_ref[:384, :] = dot(merged[:, :384], normed_one, TN).astype(BF16)
    queries_grad = dot(merged[:, 384:], normed_one, TN).astype(BF16)
    for head in range(HEADS):
        weight_ref[384 + 64 * head : 448 + 64 * head, :] = queries_grad[
            128 * head : 128 * head + 64, :
        ]
    small_ref[5:6, :] = jnp.sum(merged.astype(F32), axis=0, keepdims=True)
    loads[3].wait()
    grad_one = dot(merged, wq[...], NT)
    small_ref[0:1, :] = jnp.sum(grad_one * hat, axis=0, keepdims=True)
    small_ref[1:2, :] = jnp.sum(grad_one, axis=0, keepdims=True)
    total = tp_sum(
        norm_part[...] + grad_one * gain_one,
        my_tp,
        (tp_mine, tp_out, tp_slots, tp_gathered),
        (tp_send, tp_recv),
    )
    hat, inverse = centre(resid_ref[...])
    along = jnp.mean(total * hat, axis=-1, keepdims=True)
    level = jnp.mean(total, axis=-1, keepdims=True)
    out_ref[...] = grad_ref[...] + inverse * (total - level - hat * along)

    @pl.loop(0, me)
    def _(target):
        term_copy(target).wait_send()


def backward(layer, grad, residual, vec, rot, saved, wq, wp, wu, wd):
    return pl.pallas_call(
        functools.partial(backward_kernel, layer),
        name=f"layer_backward_{layer}",
        out_shape=[
            jax.ShapeDtypeStruct((ROWS, D), F32),
            jax.ShapeDtypeStruct((GRAD_ROWS, D), BF16),
            jax.ShapeDtypeStruct((8, D), F32),
        ],
        in_specs=vmem(10) + hbm(4),
        out_specs=vmem(3),
        scratch_shapes=[
            pltpu.VMEM((D, D), BF16),
            pltpu.VMEM((384, D), BF16),
            pltpu.VMEM((D, D), BF16),
            pltpu.VMEM((D, D), BF16),
            pltpu.VMEM((CTX * ROWS, 384), BF16),
            pltpu.VMEM((CTX, ROWS, 384), BF16),
            pltpu.VMEM((HEADS, 2 * ROWS, 128), BF16),
            pltpu.VMEM((HEADS, 2 * ROWS, 128), BF16),
            pltpu.VMEM((HEADS, ROWS, 128), F32),
            pltpu.VMEM((8, ROWS), F32),
            pltpu.VMEM((ROWS, D), F32),
            pltpu.SemaphoreType.DMA((4,)),
            pltpu.SemaphoreType.DMA((CTX,)),
            pltpu.SemaphoreType.DMA((CTX,)),
            *TP_BUFFERS,
            *TP_SEMS,
        ],
        compiler_params=pltpu.CompilerParams(
            collective_id=2 + layer, has_side_effects=True, vmem_limit_bytes=56 << 20
        ),
    )(grad, residual, vec, rot, *saved, wq, wp, wu, wd)


RING = 4
BIG = GRAD_ROWS // RING
SUB = BIG // RING
BIG_CUT, SUB_CUT = 288, 80
HALF = D // 2
RS_MESSAGES, AG_MESSAGES = 6, 6
FLOW_SEMS = 2 * RS_MESSAGES + 1 + 2 * AG_MESSAGES


def rows_at(start, count):
    return pl.ds(pl.multiple_of(start, 16), count)


class Axis:
    def __init__(self, place, of_place):
        self.place = place
        self.of_place = of_place
        self.right = of_place(lax.rem(place + 1, RING))
        self.left = of_place(lax.rem(place + 3, RING))

    def at(self, step):
        return lax.rem(self.place + step + RING, RING)


class ReduceScatter:
    def __init__(self, axis, src, size, cut, first, second, from_left, from_right, sems):
        self.axis, self.src, self.size, self.cut = axis, src, size, cut
        self.first, self.second = first, second
        self.from_left, self.from_right = from_left, from_right
        self.send, self.recv, self.base = sems

    def copy(self, index, src, dst, ctx):
        return remote(
            src, dst, self.send.at[self.base + index], self.recv.at[self.base + index], ctx=ctx
        )

    def copies(self):
        axis, size, cut = self.axis, self.size, self.cut
        rest = size - cut
        far, near_right, near_left = axis.at(2) * size, axis.at(1) * size, axis.at(3) * size
        return [
            self.copy(0, self.src(far, cut), self.first[0].at[pl.ds(0, cut)], axis.right),
            self.copy(1, self.src(far + cut, rest), self.second[0].at[pl.ds(0, rest)], axis.left),
            self.copy(
                2, self.src(near_right + cut, rest), self.from_left.at[pl.ds(cut, rest)], axis.right
            ),
            self.copy(3, self.src(near_left, cut), self.from_right.at[pl.ds(0, cut)], axis.left),
            self.copy(
                4, self.first[1].at[pl.ds(0, cut)], self.from_left.at[pl.ds(0, cut)], axis.right
            ),
            self.copy(
                5, self.second[1].at[pl.ds(0, rest)], self.from_right.at[pl.ds(cut, rest)], axis.left
            ),
        ]

    def start(self):
        for copy in self.copies()[:4]:
            copy.start()

    def middle(self):
        axis, size, cut = self.axis, self.size, self.cut
        rest = size - cut
        copies = self.copies()
        copies[0].wait_recv()
        self.first[1][0:cut, :] = (
            self.first[0][0:cut, :].astype(F32) + self.src(axis.at(1) * size, cut)[...].astype(F32)
        ).astype(BF16)
        copies[4].start()
        copies[1].wait_recv()
        self.second[1][0:rest, :] = (
            self.second[0][0:rest, :].astype(F32)
            + self.src(axis.at(3) * size + cut, rest)[...].astype(F32)
        ).astype(BF16)
        copies[5].start()

    def finish(self, out):
        for copy in self.copies()[2:]:
            copy.wait_recv()
        size = self.size
        out[0:size, :] = (
            self.src(self.axis.place * size, size)[...].astype(F32)
            + self.from_left[0:size, :].astype(F32)
            + self.from_right[0:size, :].astype(F32)
        ).astype(BF16)

    def drain(self):
        for copy in self.copies():
            copy.wait_send()


class AllGather:
    def __init__(self, axis, view, size, cut, sems):
        self.axis, self.view, self.size, self.cut = axis, view, size, cut
        self.send, self.recv, self.base = sems

    def copy(self, index, start, count, ctx):
        part = self.view(start, count)
        return remote(
            part, part, self.send.at[self.base + index], self.recv.at[self.base + index], ctx=ctx
        )

    def copies(self, shift):
        axis, size, cut = self.axis, self.size, self.cut
        rest = size - cut
        if shift == 0:
            own, from_left, from_right = axis.place * size, axis.at(3) * size, axis.at(1) * size
            return [
                self.copy(0, own, cut, axis.right),
                self.copy(1, own + cut, rest, axis.left),
                self.copy(2, own + cut, rest, axis.right),
                self.copy(3, own, cut, axis.left),
                self.copy(4, from_left, cut, axis.right),
                self.copy(5, from_right + cut, rest, axis.left),
            ]
        from_left, from_right, far = axis.at(3) * size, axis.at(1) * size, axis.at(2) * size
        return [
            self.copy(0, from_left, cut, axis.right),
            self.copy(1, from_right + cut, rest, axis.left),
            self.copy(2, from_left + cut, rest, axis.right),
            self.copy(3, from_right, cut, axis.left),
            self.copy(4, far, cut, axis.right),
            self.copy(5, far + cut, rest, axis.left),
        ]

    def start(self):
        for copy in self.copies(0)[:4]:
            copy.start()

    def middle(self):
        come, go = self.copies(1), self.copies(0)
        come[0].wait_recv()
        go[4].start()
        come[1].wait_recv()
        go[5].start()

    def finish(self):
        for copy in self.copies(1)[2:]:
            copy.wait_recv()

    def drain(self):
        for copy in self.copies(0):
            copy.wait_send()


FLOW_BUFFERS = [
    pltpu.VMEM((BIG_CUT, HALF), BF16),
    pltpu.VMEM((BIG_CUT, HALF), BF16),
    pltpu.VMEM((BIG - BIG_CUT, HALF), BF16),
    pltpu.VMEM((BIG - BIG_CUT, HALF), BF16),
    pltpu.VMEM((BIG, HALF), BF16),
    pltpu.VMEM((BIG, HALF), BF16),
    pltpu.VMEM((BIG, HALF), BF16),
    pltpu.VMEM((SUB_CUT, HALF), BF16),
    pltpu.VMEM((SUB_CUT, HALF), BF16),
    pltpu.VMEM((SUB - SUB_CUT, HALF), BF16),
    pltpu.VMEM((SUB - SUB_CUT, HALF), BF16),
    pltpu.VMEM((SUB, HALF), BF16),
    pltpu.VMEM((SUB, HALF), BF16),
    pltpu.VMEM((SUB, HALF), BF16),
    pltpu.VMEM((SUB, HALF), BF16),
    pltpu.SemaphoreType.DMA((FLOW_SEMS,)),
    pltpu.SemaphoreType.DMA((FLOW_SEMS,)),
]


class Flow:
    def __init__(self, axes, across, src_ref, out_ref, half, scratch):
        one, two = axes
        (a0, a1, b0, b1, left, right, self.big, c0, c1, d0, d1, left2, right2, self.sub, self.other) = (
            scratch[:15]
        )
        self.send, self.recv = scratch[15:]
        lanes = pl.ds(half * HALF, HALF)

        def src(start, count):
            return src_ref.at[rows_at(start, count), lanes]

        def middle_src(start, count):
            return self.big.at[rows_at(start, count)]

        def out(start, count):
            return out_ref.at[rows_at(start, count), lanes]

        corner = one.place * BIG

        def out_sub(start, count):
            return out_ref.at[rows_at(corner + start, count), lanes]

        self.out_piece = out_sub(two.place * SUB, SUB)
        self.across = across

        def sems(base):
            return (self.send, self.recv, base)

        self.one = ReduceScatter(one, src, BIG, BIG_CUT, (a0, a1), (b0, b1), left, right, sems(0))
        self.two = ReduceScatter(
            two, middle_src, SUB, SUB_CUT, (c0, c1), (d0, d1), left2, right2, sems(6)
        )
        self.three = AllGather(two, out_sub, SUB, SUB_CUT, sems(13))
        self.four = AllGather(one, out, BIG, BIG_CUT, sems(19))

    def swap(self):
        return remote(self.sub, self.other, self.send.at[12], self.recv.at[12], ctx=self.across)

    def step(self, number):
        if number == 0:
            self.one.start()
        elif number == 1:
            self.one.middle()
        elif number == 2:
            self.one.finish(self.big)
            self.two.start()
        elif number == 3:
            self.two.middle()
        elif number == 4:
            self.two.finish(self.sub)
            self.swap().start()
        elif number == 5:
            self.swap().wait_recv()
            self.out_piece[...] = (
                self.sub[...].astype(F32) + self.other[...].astype(F32)
            ).astype(BF16)
            self.three.start()
        elif number == 6:
            self.three.middle()
        elif number == 7:
            self.three.finish()
            self.four.start()
        elif number == 8:
            self.four.middle()
        elif number == 9:
            self.four.finish()

    def drain(self):
        self.one.drain()
        self.two.drain()
        self.swap().wait_send()
        self.three.drain()
        self.four.drain()


STEPS = 10


def reduce_kernel(w0, w1, s0, s1, o0, o1, small_out, small, small_slots, small_send, small_recv, *flow):
    me = lax.axis_index("ctx")
    my_tp = lax.axis_index("tp")
    z = lax.rem(me, 4)
    x = lax.rem(me // 4, 2)
    y = me // 8
    across = me + 4 - 8 * x
    z_axis = Axis(z, lambda place: me - z + place)
    y_axis = Axis(y, lambda place: me + (place - y) * 8)
    z_peers = [z_axis.of_place(z_axis.at(step)) for step in (1, 2, 3)]
    y_peers = [y_axis.of_place(y_axis.at(step)) for step in (1, 2, 3)]
    tp_peers = [lax.rem(my_tp + step, TP) for step in (1, 2, 3)]
    barrier, count = greet(z_peers + y_peers + [across], tp_peers)
    pl.semaphore_wait(barrier, count)

    flows = []
    per = len(FLOW_BUFFERS)
    for index, (src, out, half) in enumerate(((w1, o1, 0), (w1, o1, 1), (w0, o0, 0), (w0, o0, 1))):
        axes = (z_axis, y_axis) if half == 0 else (y_axis, z_axis)
        flows.append(Flow(axes, across, src, out, half, flow[per * index : per * index + per]))

    def small_copies(stage, place, peers, tp):
        return [
            remote(
                small.at[stage],
                small_slots.at[stage, place],
                small_send.at[stage, step],
                small_recv.at[stage, step],
                **({"tp": peer} if tp else {"ctx": peer}),
            )
            for step, peer in enumerate(peers)
        ]

    stages = [
        small_copies(0, z, z_peers, False),
        small_copies(1, y, y_peers, False),
        small_copies(2, x, [across], False),
        small_copies(3, my_tp, tp_peers, True),
    ]
    places = (z, y, x, my_tp)

    def small_total(stage):
        for copy in stages[stage]:
            copy.wait_recv()
        small_slots[stage, places[stage]] = small[stage]
        total = small_slots[stage, 0]
        for place in range(1, 2 if stage == 2 else 4):
            total = total + small_slots[stage, place]
        return total

    def small_step(number):
        if number == 0:
            small[0, 0:8, :] = s0[...]
            small[0, 8:16, :] = s1[...]
        elif number < 4:
            small[number] = small_total(number - 1)
        if number < 4:
            for copy in stages[number]:
                copy.start()
        elif number == 4:
            total = small_total(3)
            row = lax.rem(lax.broadcasted_iota(jnp.int32, (16, D), 0), 8)
            small_out[...] = jnp.where(row < 4, total, small[3])

    for number in range(STEPS):
        if number < 5:
            small_step(number)
        for one in flows:
            one.step(number)
    for one in flows:
        one.drain()
    for copies in stages:
        for copy in copies:
            copy.wait_send()


def reduce_all(w0, w1, s0, s1):
    return pl.pallas_call(
        reduce_kernel,
        name="weight_gradient_sum",
        out_shape=[
            jax.ShapeDtypeStruct((GRAD_ROWS, D), BF16),
            jax.ShapeDtypeStruct((GRAD_ROWS, D), BF16),
            jax.ShapeDtypeStruct((16, D), F32),
        ],
        in_specs=vmem(4),
        out_specs=vmem(3),
        scratch_shapes=[
            pltpu.VMEM((4, 16, D), F32),
            pltpu.VMEM((4, 4, 16, D), F32),
            pltpu.SemaphoreType.DMA((4, 3)),
            pltpu.SemaphoreType.DMA((4, 3)),
            *(FLOW_BUFFERS * 4),
        ],
        compiler_params=pltpu.CompilerParams(
            collective_id=4, has_side_effects=True, vmem_limit_bytes=56 << 20
        ),
    )(w0, w1, s0, s1)


def rotary_planes(positions):
    halves = ROT // 2
    inverse = jnp.power(10000.0, -2.0 * jnp.arange(halves, dtype=F32) / ROT)
    angles = positions[:, None] * inverse[None, :]
    cosine, sine = jnp.cos(angles), jnp.sin(angles)
    rows = positions.shape[0]
    rest = 128 - ROT
    return jnp.stack(
        [
            jnp.concatenate([cosine, cosine, jnp.ones((rows, rest), F32)], axis=1),
            jnp.concatenate(
                [jnp.zeros((rows, halves), F32), sine, jnp.zeros((rows, rest), F32)], axis=1
            ),
            jnp.concatenate([-sine, jnp.zeros((rows, halves + rest), F32)], axis=1),
        ]
    )


def packed_qkv(array):
    lead = array.shape[:-2]
    parts = array.reshape(*lead, 3, HEADS, HD)
    pairs = jnp.stack([parts[..., 1, :, :], parts[..., 2, :, :]], axis=-2)
    queries = jnp.stack([parts[..., 0, :, :], jnp.zeros_like(parts[..., 0, :, :])], axis=-2)
    return jnp.concatenate(
        [pairs.reshape(*lead, 2 * HEADS * HD), queries.reshape(*lead, 2 * HEADS * HD)], axis=-1
    )


def on_device(
    layer_input,
    attention_gain,
    attention_shift,
    feedforward_gain,
    feedforward_shift,
    query_key_value_weight,
    query_key_value_bias,
    attention_out_weight,
    dense_bias,
    expand_weight,
    expand_bias,
    down_weight,
    down_bias,
    output_grad,
):
    me = lax.axis_index("ctx")
    positions = (me * ROWS + jnp.arange(ROWS, dtype=jnp.int32)).astype(F32)
    rot = rotary_planes(positions)
    vec = jnp.stack(
        [
            attention_gain.astype(F32),
            attention_shift.astype(F32),
            feedforward_gain.astype(F32),
            feedforward_shift.astype(F32),
            expand_bias.astype(F32),
            dense_bias.astype(F32) + down_bias.astype(F32),
            packed_qkv(query_key_value_bias.astype(F32)),
            jnp.zeros((LAYERS, D), F32),
        ],
        axis=1,
    )
    wq = packed_qkv(query_key_value_weight)
    wp = jnp.pad(
        attention_out_weight.reshape(LAYERS, HEADS, HD, D), ((0, 0), (0, 0), (HD, 0), (0, 0))
    ).reshape(LAYERS, 2 * HEADS * HD, D)
    residual = layer_input[0].astype(F32)
    residuals, saved = [], []
    for layer in range(LAYERS):
        residuals.append(residual)
        residual, *kept = forward(
            layer, residual, vec, rot, wq, attention_out_weight, expand_weight, down_weight
        )
        saved.append(kept)
    output = residual.astype(BF16)
    grad = output_grad[0].astype(F32)
    weights, smalls = [None] * LAYERS, [None] * LAYERS
    for layer in reversed(range(LAYERS)):
        grad, weights[layer], smalls[layer] = backward(
            layer,
            grad,
            residuals[layer],
            vec,
            rot,
            saved[layer],
            wq,
            wp,
            expand_weight,
            down_weight,
        )
    total_0, total_1, small = reduce_all(weights[0], weights[1], smalls[0], smalls[1])
    small = small.reshape(LAYERS, 8, D)
    totals = (total_0, total_1)

    def qkv_grad(total):
        pairs = total[:384].reshape(HEADS, 2, HD, D)
        queries = total[384:QKV_ROWS].reshape(1, HEADS, HD, D)
        slots = jnp.concatenate([queries, pairs.transpose(1, 0, 2, 3)], axis=0)
        return slots.reshape(3 * HEADS * HD, D).T.reshape(D, 3, HEADS * HD)

    def part(start, count):
        return jnp.stack([total[start : start + count] for total in totals]).astype(F32)

    bias = small[:, 5]
    pairs = bias[:, :384].reshape(LAYERS, HEADS, 2, HD)
    queries = bias[:, 384:].reshape(LAYERS, HEADS, 2, HD)[:, :, 0]
    merged_bias_grad = jnp.stack([queries, pairs[:, :, 0], pairs[:, :, 1]], axis=1).reshape(
        LAYERS, 3, HEADS * HD
    )
    return (
        output[None],
        grad[None],
        small[:, 0],
        small[:, 1],
        small[:, 2],
        small[:, 3],
        jnp.stack([qkv_grad(total) for total in totals]).astype(F32),
        merged_bias_grad,
        part(QKV_ROWS, OUT_ROWS),
        small[:, 4],
        part(QKV_ROWS + OUT_ROWS, UP_ROWS),
        small[:, 6],
        part(QKV_ROWS + OUT_ROWS + UP_ROWS, DOWN_ROWS),
        small[:, 4],
    )


def solution(mesh):
    in_specs = (
        P(None, "ctx", None),
        P(),
        P(),
        P(),
        P(),
        P(None, None, None, "tp"),
        P(None, None, "tp"),
        P(None, "tp", None),
        P(),
        P(None, None, "tp"),
        P(None, "tp"),
        P(None, "tp", None),
        P(),
        P(None, "ctx", None),
    )
    out_specs = (
        P(None, "ctx", None),
        P(None, "ctx", None),
        P(),
        P(),
        P(),
        P(),
        P(None, None, None, "tp"),
        P(None, None, "tp"),
        P(None, "tp", None),
        P(),
        P(None, None, "tp"),
        P(None, "tp"),
        P(None, "tp", None),
        P(),
    )
    return jax.shard_map(
        on_device, mesh=mesh, in_specs=in_specs, out_specs=out_specs, check_vma=False
    )
```

time: 2410 us -> 451 us (0.19)
  waiting for transfers between devices: 1230 us -> 0 us
  blocking collectives: 893 us -> 0 us
  Pallas kernels: 0 us -> 400 us
  matrix products: 88.5 us -> 0 us
  local copies, waits for them, and re-layouts: 107 us -> 31.5 us
  other arithmetic: 53.8 us -> 17.3 us
    unnamed x16 -> x0, waiting for transfers between devices: 967 us -> none
    all_gather x8 -> x0, blocking collectives: 709 us -> none  [the longest x1 93.5 us: on_device(): lax.all_gather(shares[6].astype(jnp.bfloat16), 'ctx', axis=2, tiled=True)]
    pallas_call x0 -> x5, Pallas kernels: none -> 400 us  [the longest x2 159 us: backward(): pl.pallas_call(functools.partial(backward_kernel, layer), name=f'layer_ba...]
    unnamed x1 -> x0, blocking collectives: 184 us -> none
    all_gather x5 -> x0, waiting for transfers between devices: 161 us -> none  [the longest x2 161 us: forward_attention(): piece = lax.all_gather(key_value, 'ctx', axis=1, tiled=True)]
    psum x3 -> x0, waiting for transfers between devices: 105 us -> none  [the longest x2 72.1 us: on_device(): lax.psum(normed_two_grad.astype(jnp.bfloat16), 'tp').astype(jnp.float32)]
    dot_general x34 -> x0, matrix products: 85.7 us -> none  [the longest x4 17.3 us: compute(): jnp.einsum('sqhd,skhd->shqk', queries, keys, preferred_element_type=jnp.f...]
    unnamed x242 -> x52, local copies, waits for them, and re-layouts: 74.8 us -> 7.81 us
  transfers between devices with their start and end apart: 12 -> 0, of which waited for: 9 -> 0; matrix products, arithmetic and copies ran while one was open for 5% -> 0% of each run, Pallas kernels for 0% -> 0%
where the time goes in v1:
time: 451 us; the launch traced here: 450 us
  Pallas kernels  400 us (89%)
  local copies, waits for them, and re-layouts  31.5 us (7%)
  other arithmetic  17.3 us (4%)
    pallas_call x2, Pallas kernels, backward(): pl.pallas_call(functools.partial(backward_kernel, layer), name=f'layer_ba...  159 us
    pallas_call x2, Pallas kernels, forward(): pl.pallas_call(functools.partial(forward_kernel, layer), name=f'layer_for...  125 us
    pallas_call x1, Pallas kernels, reduce_all(): pl.pallas_call(reduce_kernel, name='weight_gradient_sum', out_shape=[jax....  117 us

profile of v1, /device:TPU:0, one launch (start us, length us, event | category | flops | bytes accessed | tf_op | source)
XLA Modules:
  0.0 450.3 jit_solution(3660210626059884128)
XLA Ops:
  0.7 1.1 bitcast_convert_fusion.1.resid_ref
  7.8 1.2 slice_bitcast_fusion.6
  9.8 1.4 pad_maximum_fusion.1
  11.1 1.4 copy.73
  12.6 1.5 pad_maximum_fusion.wq_hbm
  14.1 55.3 %layer_forward_0.1 = (f32[128,768]{1,0:T(8,128)S(1)}, bf16[4096,384]{1,0:T(8,128)(2,1)}, bf16[128,384]{1,0:T(8,128)(2,1)S(1)}, f32[192,128]{1,0:T(8,128)S(1)}, f...) custom-call(f32[128,768]{1,0:T(8,128)S(1)} %bitcast_convert_fusion.1.resid_ref, ...), custom_call_target="tpu_custom_call" | custom-call | tf_op jit(solution)/shard_map/layer_forward_0/pallas_call | solution.py:298
  72.1 69.3 %layer_forward_1.1 = (f32[128,768]{1,0:T(8,128)S(1)}, bf16[4096,384]{1,0:T(8,128)(2,1)}, bf16[128,384]{1,0:T(8,128)(2,1)S(1)}, f32[192,128]{1,0:T(8,128)S(1)}, f...) custom-call(f32[128,768]{1,0:T(8,128)S(1)} %get-tuple-element.37.resid_ref, ...), custom_call_target="tpu_custom_call" | custom-call | tf_op jit(solution)/shard_map/layer_forward_1/pallas_call | solution.py:298
  141.4 0.8 convert_bitcast_fusion
  142.2 0.8 bitcast_convert_fusion.grad_ref
  143.0 1.1 pad.7
  144.1 75.6 %layer_backward_1.1 = (f32[128,768]{1,0:T(8,128)}, bf16[2304,768]{1,0:T(8,128)(2,1)}, f32[8,768]{1,0:T(8,128)}) custom-call(f32[128,768]{1,0:T(8,128)} %bitcast_convert_fusion.grad_ref, f32[128,768]{1,0:T(8,128)} %copy-done.4, f32[2,8,768]{2,1,0:T(8,128)} %copy-done.5, f32[3,128,128]{2,1,0:T(8,128)} %copy-done.2, ...), custom_call_target="tpu_custom_call" | custom-call | tf_op jit(solution)/shard_map/layer_backward_1/pallas_call | solution.py:498
  219.8 83.0 %layer_backward_0.1 = (f32[128,768]{1,0:T(8,128)}, bf16[2304,768]{1,0:T(8,128)(2,1)}, f32[8,768]{1,0:T(8,128)}) custom-call(f32[128,768]{1,0:T(8,128)} %get-tuple-element.45.grad_ref, f32[128,768]{1,0:T(8,128)} %copy-done.3, f32[2,8,768]{2,1,0:T(8,128)} %copy-done.5, f32[3,128,128]{2,1,0:T(8,128)} %copy-done.2, bf16[4096,384]{1,0:T(8,128)(2,1)} %get-tuple-element.46.kv_ref, ...), custom_call_target="tpu_custom_call" | custom-call | tf_op jit(solution)/shard_map/layer_backward_0/pallas_call | solution.py:498
  302.8 117.2 %weight_gradient_sum.1 = (bf16[2304,768]{1,0:T(8,128)(2,1)}, bf16[2304,768]{1,0:T(8,128)(2,1)}, f32[16,768]{1,0:T(8,128)}) custom-call(bf16[2304,768]{1,0:T(8,128)(2,1)} %get-tuple-element.53.w0, bf16[2304,768]{1,0:T(8,128)(2,1)} %get-tuple-element.54.w1, f32[8,768]{1,0:T(8,128)} %get-tuple-element.55.s0, f32[8,768]{1,0:T(8,128)} %get-tuple-element.56.s1), custom_call_target="tpu_custom_call" | custom-call | tf_op jit(solution)/shard_map/weight_gradient_sum/pallas_call | solution.py:853
  420.0 1.8 fusion.1
  424.2 1.1 slice.98
  425.4 2.0 slice_bitcast_fusion.7
  428.4 2.0 maximum_convert_fusion.2
  433.2 1.3 stack.125
  434.5 1.4 reshape.119
  437.3 1.3 pad_maximum_fusion.7
  438.6 2.1 maximum_convert_fusion.3
  441.4 1.8 slice_bitcast_fusion
  443.4 2.5 maximum_convert_fusion
  446.4 2.5 maximum_convert_fusion.1
  (97 shorter events, 19.8 us)
Async XLA Ops:
  0.6 7.1 %copy-start.17 = (bf16[2,768,3,192]{1,3,2,0:T(8,128)(2,1)S(1)}, bf16[2,768,3,192]{1,3,2,0:T(8,128)(2,1)}, u32[]{:S(2)}) copy-start(bf16[2,768,3,192]{1,3,2,0:T(8,128)(2,1)} %param.19) | copy-start | bytes 5308420
  1.7 12.3 %copy-start.3 = (f32[128,768]{1,0:T(8,128)}, f32[128,768]{1,0:T(8,128)S(1)}, u32[]{:S(2)}) copy-start(f32[128,768]{1,0:T(8,128)S(1)} %bitcast_convert_fusion.1.resid_ref) | copy-start | bytes 1179652
  7.1 65.0 %copy-start.5 = (f32[2,8,768]{2,1,0:T(8,128)}, f32[2,8,768]{2,1,0:T(8,128)S(1)}, u32[]{:S(2)}) copy-start(f32[2,8,768]{2,1,0:T(8,128)S(1)} %stack.116.vec_ref) | copy-start | bytes 147460
  7.7 64.3 %copy-start.2 = (f32[3,128,128]{2,1,0:T(8,128)}, f32[3,128,128]{2,1,0:T(8,128)S(1)}, u32[]{:S(2)}) copy-start(f32[3,128,128]{2,1,0:T(8,128)S(1)} %pad_maximum_fusion.4.rot_ref) | copy-start | bytes 589828
  12.6 1.5 copy-start.1
  14.1 57.9 %copy-start = (bf16[2,768,768]{2,1,0:T(8,128)(2,1)}, bf16[2,768,768]{2,1,0:T(8,128)(2,1)S(1)}, u32[]{:S(2)}) copy-start(bf16[2,768,768]{2,1,0:T(8,128)(2,1)S(1)} %pad_maximum_fusion.wq_hbm) | copy-start | bytes 7077892
  69.4 0.8 copy-start.6
  70.2 0.7 copy-start.10
  70.8 0.6 copy-start.11
  71.4 0.6 copy-start.14
  72.0 69.3 %copy-start.4 = (f32[128,768]{1,0:T(8,128)}, f32[128,768]{1,0:T(8,128)S(1)}, u32[]{:S(2)}) copy-start(f32[128,768]{1,0:T(8,128)S(1)} %get-tuple-element.37.resid_ref) | copy-start | bytes 1179652
  72.0 69.3 %copy-start.8 = (bf16[128,768]{1,0:T(8,128)(2,1)}, bf16[128,768]{1,0:T(8,128)(2,1)S(1)}, u32[]{:S(2)}) copy-start(bf16[128,768]{1,0:T(8,128)(2,1)S(1)} %get-tuple-element.51.hid_ref) | copy-start | bytes 589828
  72.0 70.2 %copy-start.19 = (bf16[1,128,768]{2,1,0:T(8,128)(2,1)S(1)}, bf16[1,128,768]{2,1,0:T(8,128)(2,1)}, u32[]{:S(2)}) copy-start(bf16[1,128,768]{2,1,0:T(8,128)(2,1)} %param.27) | copy-start | bytes 589828
  141.4 2.7 copy-start.7
  141.4 2.7 copy-start.9
  141.4 2.7 copy-start.12
  141.4 2.7 copy-start.13
  141.4 2.7 copy-start.15
  425.3 2.2 copy-start.16
  441.4 7.5 %copy-start.20 = (f32[2,1,768]{2,0,1:T(2,128)}, f32[2,1,768]{2,0,1:T(2,128)S(1)}, u32[]{:S(2)}) copy-start(f32[2,1,768]{2,0,1:T(2,128)S(1)} %copy.104) | copy-start | bytes 18436
  446.4 3.1 copy-start.18

commit v2 on v1

--- a/solution.py
+++ b/solution.py
@@ -20,8 +20,10 @@
 HEADS = 3
 CTX = 32
 TP = 4
-CHUNK = 512
-PER = CHUNK // ROWS
+RING = 4
+GROUPS = CTX // RING
+KEYS = RING * ROWS
+WIDE = HEADS * HD
 QUARTER = ROWS // TP
 SCALE = HD**-0.5
 G1, S1, G2, S2, BUP, BOUT, BQKV = range(7)
@@ -66,26 +68,11 @@
     return barrier, len(ctx_peers) + len(tp_peers)
 
 
-def greet_all(me, my_tp):
-    barrier = pltpu.get_barrier_semaphore()
-
-    @pl.loop(1, CTX)
-    def _(step):
-        pl.semaphore_signal(
-            barrier,
-            inc=1,
-            device_id={"ctx": lax.rem(me + step, CTX)},
-            device_id_type=pl.DeviceIdType.MESH,
-        )
-
-    for step in range(1, TP):
-        pl.semaphore_signal(
-            barrier,
-            inc=1,
-            device_id={"tp": lax.rem(my_tp + step, TP)},
-            device_id_type=pl.DeviceIdType.MESH,
-        )
-    return barrier
+def greet_layer(me, my_tp):
+    z, group = lax.rem(me, RING), me // RING
+    ring = [group * RING + lax.rem(z + step, RING) for step in range(1, RING)]
+    column = [lax.rem(group + step, GROUPS) * RING + z for step in range(1, GROUPS)]
+    return greet(ring + column, [lax.rem(my_tp + step, TP) for step in range(1, TP)])
 
 
 def centre(residual):
@@ -161,6 +148,24 @@
 TP_SEMS = [pltpu.SemaphoreType.DMA((2 * TP - 2,)), pltpu.SemaphoreType.DMA((2 * TP - 2,))]
 
 
+def group_copies(buffer, stats, here, there, group, z, sems):
+    send, recv, stat_send, stat_recv = sems
+    target = group * RING + z
+    main = remote(
+        buffer[0].at[here], buffer[1].at[there], send.at[group], recv.at[there], ctx=target
+    )
+    side = remote(
+        stats[0].at[here], stats[1].at[there], stat_send.at[group], stat_recv.at[there], ctx=target
+    )
+    return main, side
+
+
+def allowed_pairs(group, of_query, z):
+    key_pos = group * KEYS + lax.broadcasted_iota(jnp.int32, (KEYS, ROWS), 0)
+    query_pos = of_query * KEYS + z * ROWS + lax.broadcasted_iota(jnp.int32, (KEYS, ROWS), 1)
+    return key_pos <= query_pos
+
+
 def forward_kernel(
     layer,
     resid_ref,
@@ -172,7 +177,7 @@
     wd_hbm,
     next_ref,
     kv_ref,
-    qp_ref,
+    q_ref,
     att_ref,
     lse_ref,
     pre_ref,
@@ -181,11 +186,20 @@
     wo,
     wu,
     wd,
-    acc,
-    top,
+    kv_t,
+    part_out,
+    part_in,
+    lse_out,
+    lse_in,
     load_sem,
     kv_send,
     kv_recv,
+    q_send,
+    q_recv,
+    part_send,
+    part_recv,
+    lse_send,
+    lse_recv,
     tp_mine,
     tp_out,
     tp_slots,
@@ -195,12 +209,13 @@
 ):
     me = lax.axis_index("ctx")
     my_tp = lax.axis_index("tp")
+    z, group = lax.rem(me, RING), me // RING
     loads = []
     for index, (src, dst) in enumerate(((wq_hbm, wq), (wu_hbm, wu), (wd_hbm, wd), (wo_hbm, wo))):
         load = pltpu.make_async_copy(src.at[layer], dst, load_sem.at[index])
         load.start()
         loads.append(load)
-    barrier = greet_all(me, my_tp)
+    barrier, count = greet_layer(me, my_tp)
 
     residual = resid_ref[...]
     vec = vec_ref.at[layer]
@@ -208,21 +223,42 @@
     normed = (hat * vec[G1 : G1 + 1, :] + vec[S1 : S1 + 1, :]).astype(BF16)
     loads[0].wait()
     merged = dot(normed, wq[...]) + vec[BQKV : BQKV + 1, :]
-    merged = turn(merged, rot_ref, 1.0).astype(BF16)
-    own = pl.ds(pl.multiple_of(me * ROWS, ROWS), ROWS)
-    kv_ref[own, :] = merged[:, :384]
-    qp_ref[...] = merged[:, 384:]
-    pl.semaphore_wait(barrier, CTX - 1 + TP - 1)
-
-    @pl.loop(me + 1, CTX)
+    merged = turn(merged, rot_ref, 1.0)
+
+    def ring_rows(step):
+        place = lax.rem(z + step + RING, RING)
+        return pl.ds(pl.multiple_of(place * ROWS, ROWS), ROWS)
+
+    def kv_copy(step):
+        own = ring_rows(0)
+        return remote(
+            kv_ref.at[own],
+            kv_ref.at[own],
+            kv_send.at[step - 1],
+            kv_recv.at[step - 1],
+            ctx=group * RING + lax.rem(z + step, RING),
+        )
+
+    def q_copy(target, source):
+        return remote(
+            q_ref.at[source],
+            q_ref.at[source],
+            q_send.at[target],
+            q_recv.at[source],
+            ctx=target * RING + z,
+        )
+
+    kv_ref[ring_rows(0), :] = merged[:, :384].astype(BF16)
+    for head in range(HEADS):
+        across = merged[:, 384 + 128 * head : 512 + 128 * head].T
+        q_ref[group, HD * head : HD * head + HD, :] = across[:HD, :].astype(BF16)
+    pl.semaphore_wait(barrier, count)
+    for step in range(1, RING):
+        kv_copy(step).start()
+
+    @pl.loop(0, group)
     def _(target):
-        remote(
-            kv_ref.at[own], kv_ref.at[own], kv_send.at[target], kv_recv.at[me], ctx=target
-        ).start()
-
-    @pl.loop(me + 1, (me // PER + 1) * PER)
-    def _(block):
-        kv_ref[pl.ds(pl.multiple_of(block * ROWS, ROWS), ROWS), :] = jnp.zeros((ROWS, 384), BF16)
+        q_copy(target, group).start()
 
     normed = (hat * vec[G2 : G2 + 1, :] + vec[S2 : S2 + 1, :]).astype(BF16)
     loads[1].wait()
@@ -231,47 +267,78 @@
     hidden = (pre * (1.0 + lax.erf(pre * math.sqrt(0.5))) * 0.5).astype(BF16)
     hid_ref[...] = hidden
     loads[2].wait()
-    branch = dot(hidden, wd[...])
-    next_ref[...] = branch
-
-    acc[...] = jnp.zeros_like(acc)
-    top[...] = jnp.zeros_like(top)
-    for head in range(HEADS):
-        top[head : head + 1, :] = jnp.full((1, ROWS), MASKED, F32)
-
-    @pl.loop(0, me // PER + 1)
-    def _(chunk):
-        @pl.loop(chunk * PER, jnp.minimum(chunk * PER + PER, me))
-        def _(source):
-            rows = pl.ds(pl.multiple_of(source * ROWS, ROWS), ROWS)
-            remote(
-                kv_ref.at[rows], kv_ref.at[rows], kv_send.at[source], kv_recv.at[source], ctx=source
-            ).wait_recv()
-
-        keys = pl.ds(pl.multiple_of(chunk * CHUNK, CHUNK), CHUNK)
-        key_pos = chunk * CHUNK + lax.broadcasted_iota(jnp.int32, (CHUNK, ROWS), 0)
-        query_pos = me * ROWS + lax.broadcasted_iota(jnp.int32, (CHUNK, ROWS), 1)
-        allowed = key_pos <= query_pos
+    next_ref[...] = dot(hidden, wd[...])
+
+    for step in range(1, RING):
+        rows = ring_rows(-step)
+        remote(
+            kv_ref.at[rows],
+            kv_ref.at[rows],
+            kv_send.at[step - 1],
+            kv_recv.at[step - 1],
+            ctx=group * RING + lax.rem(z + step, RING),
+        ).wait_recv()
+    kv_t[...] = kv_ref[...].T
+
+    def attend(of_query, own):
+        allowed = allowed_pairs(group, of_query, z)
         for head in range(HEADS):
-            lanes = slice(128 * head, 128 * head + 128)
-            block = kv_ref[keys, lanes]
-            scores = dot(block, qp_ref[:, lanes], NT) * SCALE
-            scores = jnp.where(allowed, scores, MASKED)
-            old = top[head : head + 1, :]
-            new = jnp.maximum(old, jnp.max(scores, axis=0, keepdims=True))
-            weights = jnp.exp(scores - new)
-            shrink = jnp.exp(old - new)
-            top[head : head + 1, :] = new
-            top[4 + head : 5 + head, :] = top[4 + head : 5 + head, :] * shrink + jnp.sum(
-                weights, axis=0, keepdims=True
+            rows = slice(HD * head, HD * head + HD)
+            scores = dot(kv_ref[:, 128 * head : 128 * head + HD], q_ref[of_query, rows, :]) * SCALE
+            if own:
+                scores = jnp.where(allowed, scores, MASKED)
+            highest = jnp.max(scores, axis=0, keepdims=True)
+            weights = jnp.exp(scores - highest)
+            total = jnp.sum(weights, axis=0, keepdims=True)
+            values_t = kv_t[128 * head + HD : 128 * head + 128, :]
+            attended = dot(values_t, weights.astype(BF16)) / total
+            log_total = highest + jnp.log(total)
+            if own:
+                att_ref[rows, :] = attended
+                lse_ref[head : head + 1, :] = log_total
+            else:
+                part_out[of_query, rows, :] = attended.astype(BF16)
+                lse_out[of_query, head : head + 1, :] = log_total
+
+    def part_copies(here, there, target):
+        return group_copies(
+            (part_out, part_in),
+            (lse_out, lse_in),
+            here,
+            there,
+            target,
+            z,
+            (part_send, part_recv, lse_send, lse_recv),
+        )
+
+    lse_ref[...] = jnp.zeros_like(lse_ref)
+
+    @pl.loop(group + 1, GROUPS)
+    def _(of_query):
+        q_copy(of_query, of_query).wait_recv()
+        lse_out[of_query] = jnp.zeros((8, ROWS), F32)
+        attend(of_query, False)
+        for copy in part_copies(of_query, group, of_query):
+            copy.start()
+
+    attend(group, True)
+
+    @pl.loop(0, group)
+    def _(source):
+        for copy in part_copies(source, source, source):
+            copy.wait_recv()
+        old, new = lse_ref[...], lse_in[source]
+        highest = jnp.maximum(old, new)
+        old_part, new_part = jnp.exp(old - highest), jnp.exp(new - highest)
+        total = old_part + new_part
+        lse_ref[...] = highest + jnp.log(total)
+        old_part, new_part = old_part / total, new_part / total
+        for head in range(HEADS):
+            rows = slice(HD * head, HD * head + HD)
+            att_ref[rows, :] = att_ref[rows, :] * old_part[head : head + 1, :] + (
+                part_in[source, rows, :].astype(F32) * new_part[head : head + 1, :]
             )
-            acc[head] = acc[head] * shrink + dot(block, weights.astype(BF16), TN)
-
-    for head in range(HEADS):
-        total = top[4 + head : 5 + head, :]
-        att_ref[64 * head : 64 * head + 64, :] = acc[head, 64:, :] / total
-        lse_ref[head : head + 1, :] = top[head : head + 1, :] + jnp.log(total)
-    lse_ref[HEADS:, :] = jnp.zeros((8 - HEADS, ROWS), F32)
+
     loads[3].wait()
     branch = next_ref[...] + dot(att_ref[...].astype(BF16), wo[...], TN)
     branch = tp_sum(
@@ -279,11 +346,17 @@
     )
     next_ref[...] = resid_ref[...] + branch + vec[BOUT : BOUT + 1, :]
 
-    @pl.loop(me + 1, CTX)
+    for step in range(1, RING):
+        kv_copy(step).wait_send()
+
+    @pl.loop(0, group)
     def _(target):
-        remote(
-            kv_ref.at[own], kv_ref.at[own], kv_send.at[target], kv_recv.at[me], ctx=target
-        ).wait_send()
+        q_copy(target, group).wait_send()
+
+    @pl.loop(group + 1, GROUPS)
+    def _(of_query):
+        for copy in part_copies(of_query, group, of_query):
+            copy.wait_send()
 
 
 def vmem(count):
@@ -292,6 +365,18 @@
 
 def hbm(count):
     return [pl.BlockSpec(memory_space=pl.ANY)] * count
+
+
+GROUP_BUFFERS = [
+    pltpu.VMEM((GROUPS, WIDE, ROWS), BF16),
+    pltpu.VMEM((GROUPS, WIDE, ROWS), BF16),
+    pltpu.VMEM((GROUPS, 8, ROWS), F32),
+    pltpu.VMEM((GROUPS, 8, ROWS), F32),
+]
+
+
+def dma_sems(*counts):
+    return [pltpu.SemaphoreType.DMA((count,)) for count in counts]
 
 
 def forward(layer, residual, vec, rot, wq, wo, wu, wd):
@@ -300,9 +385,9 @@
         name=f"layer_forward_{layer}",
         out_shape=[
             jax.ShapeDtypeStruct((ROWS, D), F32),
-            jax.ShapeDtypeStruct((CTX * ROWS, 384), BF16),
-            jax.ShapeDtypeStruct((ROWS, 384), BF16),
-            jax.ShapeDtypeStruct((192, ROWS), F32),
+            jax.ShapeDtypeStruct((KEYS, 384), BF16),
+            jax.ShapeDtypeStruct((GROUPS, WIDE, ROWS), BF16),
+            jax.ShapeDtypeStruct((WIDE, ROWS), F32),
             jax.ShapeDtypeStruct((8, ROWS), F32),
             jax.ShapeDtypeStruct((ROWS, D), F32),
             jax.ShapeDtypeStruct((ROWS, D), BF16),
@@ -311,19 +396,17 @@
         out_specs=vmem(7),
         scratch_shapes=[
             pltpu.VMEM((D, D), BF16),
-            pltpu.VMEM((192, D), BF16),
+            pltpu.VMEM((WIDE, D), BF16),
             pltpu.VMEM((D, D), BF16),
             pltpu.VMEM((D, D), BF16),
-            pltpu.VMEM((HEADS, 128, ROWS), F32),
-            pltpu.VMEM((8, ROWS), F32),
-            pltpu.SemaphoreType.DMA((4,)),
-            pltpu.SemaphoreType.DMA((CTX,)),
-            pltpu.SemaphoreType.DMA((CTX,)),
+            pltpu.VMEM((384, KEYS), BF16),
+            *GROUP_BUFFERS,
+            *dma_sems(4, 3, 3, *[GROUPS] * 6),
             *TP_BUFFERS,
             *TP_SEMS,
         ],
         compiler_params=pltpu.CompilerParams(
-            collective_id=layer, has_side_effects=True, vmem_limit_bytes=48 << 20
+            collective_id=layer, has_side_effects=True, vmem_limit_bytes=40 << 20
         ),
     )(residual, vec, rot, wq, wo, wu, wd)
 
@@ -335,32 +418,42 @@
     vec_ref,
     rot_ref,
     kv_ref,
-    qp_ref,
+    q_ref,
     att_ref,
     lse_ref,
     pre_ref,
     hid_ref,
     wq_hbm,
-    wp_hbm,
+    wo_hbm,
     wu_hbm,
     wd_hbm,
     out_ref,
     weight_ref,
     small_ref,
     wq,
-    wp,
+    wo,
     wu,
     wd,
+    kv_t,
+    mixed,
+    stats,
+    query_out,
+    query_in,
+    pair,
     terms,
-    slots,
-    left,
-    right,
+    low_terms,
+    term_slots,
     query,
-    delta,
     norm_part,
     load_sem,
     kv_send,
     kv_recv,
+    mixed_send,
+    mixed_recv,
+    stat_send,
+    stat_recv,
+    query_send,
+    query_recv,
     tp_mine,
     tp_out,
     tp_slots,
@@ -370,65 +463,76 @@
 ):
     me = lax.axis_index("ctx")
     my_tp = lax.axis_index("tp")
+    z, group = lax.rem(me, RING), me // RING
     loads = []
-    for index, (src, dst) in enumerate(((wp_hbm, wp), (wd_hbm, wd), (wu_hbm, wu), (wq_hbm, wq))):
+    for index, (src, dst) in enumerate(((wo_hbm, wo), (wd_hbm, wd), (wu_hbm, wu), (wq_hbm, wq))):
         load = pltpu.make_async_copy(src.at[layer], dst, load_sem.at[index])
         load.start()
         loads.append(load)
-    barrier = greet_all(me, my_tp)
+    barrier, count = greet_layer(me, my_tp)
     vec = vec_ref.at[layer]
 
     low = grad_ref[...].astype(BF16)
     loads[0].wait()
-    mixed = dot(low, wp[...], NT).astype(BF16)
-    turned = dot(wp[...], low, NT).astype(BF16).astype(F32)
+    own_mixed = dot(wo[...], low, NT).astype(BF16)
+    mixed[group] = own_mixed
+    own_stats = [lse_ref[head : head + 1, :] for head in range(HEADS)]
     for head in range(HEADS):
-        lanes = slice(128 * head, 128 * head + 128)
-        left[head, :ROWS, :] = qp_ref[:, lanes]
-        left[head, ROWS:, :] = mixed[:, lanes]
-        right[head, :ROWS, :] = (qp_ref[:, lanes].astype(F32) * SCALE).astype(BF16)
-        right[head, ROWS:, :] = mixed[:, lanes]
-        delta[head : head + 1, :] = jnp.sum(
-            turned[128 * head + 64 : 128 * head + 128, :] * att_ref[64 * head : 64 * head + 64, :],
-            axis=0,
-            keepdims=True,
-        )
-    query[...] = jnp.zeros_like(query)
-    pl.semaphore_wait(barrier, CTX - 1 + TP - 1)
-
-    def term_copy(target):
-        rows = pl.ds(pl.multiple_of(target * ROWS, ROWS), ROWS)
+        rows = slice(HD * head, HD * head + HD)
+        own_stats.append(
+            jnp.sum(own_mixed[rows, :].astype(F32) * att_ref[rows, :], axis=0, keepdims=True)
+        )
+    for row, stat in enumerate(own_stats):
+        stats[group, row : row + 1, :] = stat
+    stats[group, 2 * HEADS :, :] = jnp.zeros((8 - 2 * HEADS, ROWS), F32)
+
+    def mixed_copies(entry, target):
+        return group_copies(
+            (mixed, mixed),
+            (stats, stats),
+            entry,
+            entry,
+            target,
+            z,
+            (mixed_send, mixed_recv, stat_send, stat_recv),
+        )
+
+    def query_copy(here, there, target):
         return remote(
-            terms.at[rows], slots.at[me], kv_send.at[target], kv_recv.at[me], ctx=target
-        )
-
-    @pl.loop(0, me // PER + 1)
-    def _(chunk):
-        keys = pl.ds(pl.multiple_of(chunk * CHUNK, CHUNK), CHUNK)
-        key_pos = chunk * CHUNK + lax.broadcasted_iota(jnp.int32, (CHUNK, ROWS), 0)
-        query_pos = me * ROWS + lax.broadcasted_iota(jnp.int32, (CHUNK, ROWS), 1)
-        allowed = key_pos <= query_pos
-        for head in range(HEADS):
-            lanes = slice(128 * head, 128 * head + 128)
-            block = kv_ref[keys, lanes]
-            both = dot(block, left[head], NT)
-            probs = jnp.where(
-                allowed, jnp.exp(both[:, :ROWS] * SCALE - lse_ref[head : head + 1, :]), 0.0
-            )
-            scores = (probs * (both[:, ROWS:] - delta[head : head + 1, :])).astype(BF16)
-            terms[keys, lanes] = dot(
-                jnp.concatenate([scores, probs.astype(BF16)], axis=1), right[head]
-            ).astype(BF16)
-            query[head] += dot(scores, block, TN)
-
-        @pl.loop(chunk * PER, jnp.minimum(chunk * PER + PER, me))
-        def _(target):
-            term_copy(target).start()
-
+            query_out.at[here],
+            query_in.at[there],
+            query_send.at[target],
+            query_recv.at[there],
+            ctx=target * RING + z,
+        )
+
+    def ring_rows(step):
+        place = lax.rem(z + step + RING, RING)
+        return pl.ds(pl.multiple_of(place * ROWS, ROWS), ROWS)
+
+    def term_copy(step):
+        return remote(
+            low_terms.at[ring_rows(step)],
+            term_slots.at[step - 1],
+            kv_send.at[step - 1],
+            kv_recv.at[step - 1],
+            ctx=group * RING + lax.rem(z + step, RING),
+        )
+
+    pl.semaphore_wait(barrier, count)
+
+    @pl.loop(0, group)
+    def _(target):
+        for copy in mixed_copies(group, target):
+            copy.start()
+
+    kv_t[...] = kv_ref[...].T
+    pair[...] = jnp.zeros_like(pair)
+    terms[...] = jnp.zeros_like(terms)
     small_ref[...] = jnp.zeros_like(small_ref)
     small_ref[4:5, :] = jnp.sum(grad_ref[...], axis=0, keepdims=True)
-    weight_ref[QKV_ROWS : QKV_ROWS + OUT_ROWS, :] = dot(att_ref[...].astype(BF16), low).astype(BF16)
-    weight_ref[QKV_ROWS + OUT_ROWS + UP_ROWS :, :] = dot(hid_ref[...], low, TN).astype(BF16)
+    hat, inverse = centre(resid_ref[...])
+    gain_one, gain_two = vec[G1 : G1 + 1, :], vec[G2 : G2 + 1, :]
     loads[1].wait()
     hidden_grad = dot(low, wd[...], NT)
     pre = pre_ref[...]
@@ -436,48 +540,86 @@
         -0.5 * pre * pre
     ) * (1.0 / math.sqrt(2.0 * math.pi))
     pre_grad = (hidden_grad * slope).astype(BF16)
+    tp_out[...] = pre_grad
     small_ref[6:7, :] = jnp.sum(pre_grad.astype(F32), axis=0, keepdims=True)
-    hat, inverse = centre(resid_ref[...])
-    gain_one, gain_two = vec[G1 : G1 + 1, :], vec[G2 : G2 + 1, :]
-    normed_two = (hat * gain_two + vec[S2 : S2 + 1, :]).astype(BF16)
-    weight_ref[QKV_ROWS + OUT_ROWS : QKV_ROWS + OUT_ROWS + UP_ROWS, :] = dot(
-        normed_two, pre_grad, TN
-    ).astype(BF16)
     loads[2].wait()
     grad_two = dot(pre_grad, wu[...], NT)
     small_ref[2:3, :] = jnp.sum(grad_two * hat, axis=0, keepdims=True)
     small_ref[3:4, :] = jnp.sum(grad_two, axis=0, keepdims=True)
     norm_part[...] = grad_two * gain_two
 
-    own = pl.ds(pl.multiple_of(me * ROWS, ROWS), ROWS)
-    out_ref[:, :384] = terms[own, :].astype(F32)
-
-    @pl.loop(me + 1, CTX)
+    def attend_back(of_query, own):
+        allowed = allowed_pairs(group, of_query, z)
+        for head in range(HEADS):
+            rows = slice(HD * head, HD * head + HD)
+            lanes = slice(128 * head, 128 * head + 128)
+            pair[head, :HD, :ROWS] = q_ref[of_query, rows, :]
+            pair[head, HD:, ROWS:] = mixed[of_query, rows, :]
+            both = dot(kv_ref[:, lanes], pair[head])
+            probs = jnp.exp(both[:, :ROWS] * SCALE - stats[of_query, head : head + 1, :])
+            if own:
+                probs = jnp.where(allowed, probs, 0.0)
+            scores = probs * (both[:, ROWS:] - stats[of_query, HEADS + head : HEADS + head + 1, :])
+            scores = (scores * SCALE).astype(BF16)
+            terms[:, lanes] += dot(
+                jnp.concatenate([scores, probs.astype(BF16)], axis=1), pair[head], NT
+            )
+            back = dot(kv_t[128 * head : 128 * head + HD, :], scores)
+            if own:
+                query[rows, :] = back
+            else:
+                query_out[of_query, rows, :] = back.astype(BF16)
+
+    @pl.loop(group + 1, GROUPS)
+    def _(of_query):
+        for copy in mixed_copies(of_query, of_query):
+            copy.wait_recv()
+        attend_back(of_query, False)
+        query_copy(of_query, group, of_query).start()
+
+    attend_back(group, True)
+    low_terms[...] = terms[...].astype(BF16)
+    for step in range(1, RING):
+        term_copy(step).start()
+
+    low = grad_ref[...].astype(BF16)
+    pre_grad = tp_out[...]
+    weight_ref[QKV_ROWS : QKV_ROWS + OUT_ROWS, :] = dot(att_ref[...].astype(BF16), low).astype(BF16)
+    weight_ref[QKV_ROWS + OUT_ROWS + UP_ROWS :, :] = dot(hid_ref[...], low, TN).astype(BF16)
+    hat, inverse = centre(resid_ref[...])
+    normed_two = (hat * gain_two + vec[S2 : S2 + 1, :]).astype(BF16)
+    weight_ref[QKV_ROWS + OUT_ROWS : QKV_ROWS + OUT_ROWS + UP_ROWS, :] = dot(
+        normed_two, pre_grad, TN
+    ).astype(BF16)
+
+    out_ref[:, :384] = terms[ring_rows(0), :]
+    for step in range(1, RING):
+        term_copy(step).wait_recv()
+        out_ref[:, :384] += term_slots[step - 1].astype(F32)
+
+    @pl.loop(0, group)
     def _(source):
-        remote(
-            terms.at[own], slots.at[source], kv_send.at[source], kv_recv.at[source], ctx=source
-        ).wait_recv()
-        out_ref[:, :384] += slots[source].astype(F32)
-
-    lane = lax.broadcasted_iota(jnp.int32, (ROWS, 128), 1)
+        query_copy(source, source, source).wait_recv()
+        query[...] += query_in[source].astype(F32)
+
     for head in range(HEADS):
-        out_ref[:, 384 + 128 * head : 512 + 128 * head] = jnp.where(
-            lane < HD, query[head] * SCALE, 0.0
-        )
+        across = jnp.concatenate(
+            [query[HD * head : HD * head + HD, :], jnp.zeros((HD, ROWS), F32)], axis=0
+        )
+        out_ref[:, 384 + 128 * head : 512 + 128 * head] = across.T
     merged = turn(out_ref[...], rot_ref, -1.0).astype(BF16)
-    hat, inverse = centre(resid_ref[...])
     normed_one = (hat * gain_one + vec[S1 : S1 + 1, :]).astype(BF16)
+    loads[3].wait()
+    grad_one = dot(merged, wq[...], NT)
+    small_ref[0:1, :] = jnp.sum(grad_one * hat, axis=0, keepdims=True)
+    small_ref[1:2, :] = jnp.sum(grad_one, axis=0, keepdims=True)
+    small_ref[5:6, :] = jnp.sum(merged.astype(F32), axis=0, keepdims=True)
     weight_ref[:384, :] = dot(merged[:, :384], normed_one, TN).astype(BF16)
     queries_grad = dot(merged[:, 384:], normed_one, TN).astype(BF16)
     for head in range(HEADS):
         weight_ref[384 + 64 * head : 448 + 64 * head, :] = queries_grad[
             128 * head : 128 * head + 64, :
         ]
-    small_ref[5:6, :] = jnp.sum(merged.astype(F32), axis=0, keepdims=True)
-    loads[3].wait()
-    grad_one = dot(merged, wq[...], NT)
-    small_ref[0:1, :] = jnp.sum(grad_one * hat, axis=0, keepdims=True)
-    small_ref[1:2, :] = jnp.sum(grad_one, axis=0, keepdims=True)
     total = tp_sum(
         norm_part[...] + grad_one * gain_one,
         my_tp,
@@ -489,12 +631,20 @@
     level = jnp.mean(total, axis=-1, keepdims=True)
     out_ref[...] = grad_ref[...] + inverse * (total - level - hat * along)
 
-    @pl.loop(0, me)
+    for step in range(1, RING):
+        term_copy(step).wait_send()
+
+    @pl.loop(0, group)
     def _(target):
-        term_copy(target).wait_send()
-
-
-def backward(layer, grad, residual, vec, rot, saved, wq, wp, wu, wd):
+        for copy in mixed_copies(group, target):
+            copy.wait_send()
+
+    @pl.loop(group + 1, GROUPS)
+    def _(of_query):
+        query_copy(of_query, group, of_query).wait_send()
+
+
+def backward(layer, grad, residual, vec, rot, saved, wq, wo, wu, wd):
     return pl.pallas_call(
         functools.partial(backward_kernel, layer),
         name=f"layer_backward_{layer}",
@@ -507,29 +657,30 @@
         out_specs=vmem(3),
         scratch_shapes=[
             pltpu.VMEM((D, D), BF16),
-            pltpu.VMEM((384, D), BF16),
+            pltpu.VMEM((WIDE, D), BF16),
             pltpu.VMEM((D, D), BF16),
             pltpu.VMEM((D, D), BF16),
-            pltpu.VMEM((CTX * ROWS, 384), BF16),
-            pltpu.VMEM((CTX, ROWS, 384), BF16),
-            pltpu.VMEM((HEADS, 2 * ROWS, 128), BF16),
-            pltpu.VMEM((HEADS, 2 * ROWS, 128), BF16),
-            pltpu.VMEM((HEADS, ROWS, 128), F32),
-            pltpu.VMEM((8, ROWS), F32),
+            pltpu.VMEM((384, KEYS), BF16),
+            pltpu.VMEM((GROUPS, WIDE, ROWS), BF16),
+            pltpu.VMEM((GROUPS, 8, ROWS), F32),
+            pltpu.VMEM((GROUPS, WIDE, ROWS), BF16),
+            pltpu.VMEM((GROUPS, WIDE, ROWS), BF16),
+            pltpu.VMEM((HEADS, 128, 2 * ROWS), BF16),
+            pltpu.VMEM((KEYS, 384), F32),
+            pltpu.VMEM((KEYS, 384), BF16),
+            pltpu.VMEM((RING - 1, ROWS, 384), BF16),
+            pltpu.VMEM((WIDE, ROWS), F32),
             pltpu.VMEM((ROWS, D), F32),
-            pltpu.SemaphoreType.DMA((4,)),
-            pltpu.SemaphoreType.DMA((CTX,)),
-            pltpu.SemaphoreType.DMA((CTX,)),
+            *dma_sems(4, 3, 3, *[GROUPS] * 6),
             *TP_BUFFERS,
             *TP_SEMS,
         ],
         compiler_params=pltpu.CompilerParams(
-            collective_id=2 + layer, has_side_effects=True, vmem_limit_bytes=56 << 20
+            collective_id=2 + layer, has_side_effects=True, vmem_limit_bytes=48 << 20
         ),
-    )(grad, residual, vec, rot, *saved, wq, wp, wu, wd)
-
-
-RING = 4
+    )(grad, residual, vec, rot, *saved, wq, wo, wu, wd)
+
+
 BIG = GRAD_ROWS // RING
 SUB = BIG // RING
 BIG_CUT, SUB_CUT = 288, 80
@@ -934,9 +1085,6 @@
         axis=1,
     )
     wq = packed_qkv(query_key_value_weight)
-    wp = jnp.pad(
-        attention_out_weight.reshape(LAYERS, HEADS, HD, D), ((0, 0), (0, 0), (HD, 0), (0, 0))
-    ).reshape(LAYERS, 2 * HEADS * HD, D)
     residual = layer_input[0].astype(F32)
     residuals, saved = [], []
     for layer in range(LAYERS):
@@ -957,7 +1105,7 @@
             rot,
             saved[layer],
             wq,
-            wp,
+            attention_out_weight,
             expand_weight,
             down_weight,
         )

time: 451 us -> 265 us (0.59)
  Pallas kernels: 400 us -> 225 us
  local copies, waits for them, and re-layouts: 31.5 us -> 24.8 us
    pallas_call x2, Pallas kernels: 159 us -> 68 us  [backward(): pl.pallas_call(functools.partial(backward_kernel, layer), name=f'layer_ba...]
    pallas_call x2, Pallas kernels: 125 us -> 61.2 us  [forward(): pl.pallas_call(functools.partial(forward_kernel, layer), name=f'layer_for...]
    pallas_call x1, Pallas kernels: 117 us -> 95.3 us  [reduce_all(): pl.pallas_call(reduce_kernel, name='weight_gradient_sum', out_shape=[jax....]
where the time goes in v2:
time: 265 us; the launch traced here: 264 us
  Pallas kernels  225 us (85%)
  local copies, waits for them, and re-layouts  24.8 us (9%)
  other arithmetic  13.8 us (5%)
    pallas_call x1, Pallas kernels, reduce_all(): pl.pallas_call(reduce_kernel, name='weight_gradient_sum', out_shape=[jax....  95.3 us
    pallas_call x2, Pallas kernels, backward(): pl.pallas_call(functools.partial(backward_kernel, layer), name=f'layer_ba...  68 us
    pallas_call x2, Pallas kernels, forward(): pl.pallas_call(functools.partial(forward_kernel, layer), name=f'layer_for...  61.2 us
    unnamed x26, local copies, waits for them, and re-layouts  7.44 us
    convert_element_type x3, other arithmetic, part(): jnp.stack([total[start:start + count] for total in totals]).astype(F32)  6.07 us

profile of v2, /device:TPU:0, one launch (start us, length us, event | category | flops | bytes accessed | tf_op | source)
XLA Modules:
  0.0 264.1 jit_solution(17436292569141533382)
XLA Ops:
  0.6 1.0 bitcast_convert_fusion.1.resid_ref
  5.0 0.7 convert_add_fusion
  5.8 0.8 reshape.120
  7.6 1.6 slice_bitcast_fusion.6
  9.2 1.4 copy.74
  10.8 1.4 copy.73
  12.2 2.0 pad_maximum_fusion.wq_hbm
  15.2 30.3 %layer_forward_0.1 = (f32[128,768]{1,0:T(8,128)S(1)}, bf16[512,384]{1,0:T(8,128)(2,1)S(1)}, bf16[8,192,128]{2,1,0:T(8,128)(2,1)S(1)}, f32[192,128]{1,0:T(8,128)S...) custom-call(f32[128,768]{1,0:T(8,128)S(1)} %bitcast_convert_fusion.1.resid_ref, ...), custom_call_target="tpu_custom_call" | custom-call | tf_op jit(solution)/shard_map/layer_forward_0/pallas_call | solution.py:383
  45.6 30.9 %layer_forward_1.1 = (f32[128,768]{1,0:T(8,128)S(1)}, bf16[512,384]{1,0:T(8,128)(2,1)S(1)}, bf16[8,192,128]{2,1,0:T(8,128)(2,1)S(1)}, f32[192,128]{1,0:T(8,128)S...) custom-call(f32[128,768]{1,0:T(8,128)S(1)} %get-tuple-element.37.resid_ref, ...), custom_call_target="tpu_custom_call" | custom-call | tf_op jit(solution)/shard_map/layer_forward_1/pallas_call | solution.py:383
  77.3 35.8 %layer_backward_1.1 = (f32[128,768]{1,0:T(8,128)S(1)}, bf16[2304,768]{1,0:T(8,128)(2,1)}, f32[8,768]{1,0:T(8,128)S(1)}) custom-call(f32[128,768]{1,0:T(8,128)S(1)} %bitcast_convert_fusion.grad_ref, f32[128,768]{1,0:T(8,128)S(1)} %get-tuple-element.37.resid_ref, f32[2,8,768]{2,1,0:T(8,128)S(1)} %stack.116.vec_ref, ...), custom_call_target="tpu_custom_call" | custom-call | tf_op jit(solution)/shard_map/layer_backward_1/pallas_call | solution.py:648
  113.6 32.3 %layer_backward_0.1 = (f32[128,768]{1,0:T(8,128)S(1)}, bf16[2304,768]{1,0:T(8,128)(2,1)}, f32[8,768]{1,0:T(8,128)S(1)}) custom-call(f32[128,768]{1,0:T(8,128)S(1)} %get-tuple-element.45.grad_ref, f32[128,768]{1,0:T(8,128)S(1)} %bitcast_convert_fusion.1.resid_ref, f32[2,8,768]{2,1,0:T(8,128)S(1)} %stack.116.vec_ref, ...), custom_call_target="tpu_custom_call" | custom-call | tf_op jit(solution)/shard_map/layer_backward_0/pallas_call | solution.py:648
  146.5 95.3 %weight_gradient_sum.1 = (bf16[2304,768]{1,0:T(8,128)(2,1)}, bf16[2304,768]{1,0:T(8,128)(2,1)}, f32[16,768]{1,0:T(8,128)}) custom-call(bf16[2304,768]{1,0:T(8,128)(2,1)} %get-tuple-element.53.w0, bf16[2304,768]{1,0:T(8,128)(2,1)} %get-tuple-element.54.w1, f32[8,768]{1,0:T(8,128)} %copy-done.4, f32[8,768]{1,0:T(8,128)} %copy-done.3), custom_call_target="tpu_custom_call" | custom-call | tf_op jit(solution)/shard_map/weight_gradient_sum/pallas_call | solution.py:1004
  241.8 1.2 fusion.1
  245.4 1.1 slice.98
  246.6 1.1 slice_bitcast_fusion.7
  247.8 1.1 slice.96
  248.9 1.1 slice_bitcast_fusion.8
  250.1 2.0 maximum_convert_fusion.2
  253.2 1.1 maximum_convert_fusion.3
  254.3 1.9 slice_bitcast_fusion
  256.3 0.8 copy-done.5
  257.2 2.5 maximum_convert_fusion
  260.3 2.5 maximum_convert_fusion.1
  263.4 0.7 copy.113
  (70 shorter events, 12.7 us)
Async XLA Ops:
  10.7 3.4 %copy-start.2 = (bf16[2,192,768]{2,1,0:T(8,128)(2,1)S(1)}, bf16[2,192,768]{2,1,0:T(8,128)(2,1)}, u32[]{:S(2)}) copy-start(bf16[2,192,768]{2,1,0:T(8,128)(2,1)} %wo_hbm.7) | copy-start | bytes 1769476
  12.2 2.4 copy-start
  12.2 3.1 %copy-start.1 = (bf16[2,768,768]{2,1,0:T(8,128)(2,1)S(1)}, bf16[2,768,768]{2,1,0:T(8,128)(2,1)}, u32[]{:S(2)}) copy-start(bf16[2,768,768]{2,1,0:T(8,128)(2,1)} %wd_hbm.7) | copy-start | bytes 7077892
  45.6 31.6 %copy-start.6 = (bf16[1,128,768]{2,1,0:T(8,128)(2,1)S(1)}, bf16[1,128,768]{2,1,0:T(8,128)(2,1)}, u32[]{:S(2)}) copy-start(bf16[1,128,768]{2,1,0:T(8,128)(2,1)} %param.27) | copy-start | bytes 589828
  113.0 0.6 copy-start.3
  145.9 0.6 copy-start.4
  254.3 8.5 %copy-start.7 = (f32[2,1,768]{2,0,1:T(2,128)}, f32[2,1,768]{2,0,1:T(2,128)S(1)}, u32[]{:S(2)}) copy-start(f32[2,1,768]{2,0,1:T(2,128)S(1)} %copy.104) | copy-start | bytes 18436
  254.3 2.7 %copy-start.5 = (bf16[2304,768]{1,0:T(8,128)(2,1)S(1)}, bf16[2304,768]{1,0:T(8,128)(2,1)}, u32[]{:S(2)}) copy-start(bf16[2304,768]{1,0:T(8,128)(2,1)} %get-tuple-element.58) | copy-start | bytes 10616836

commit v3 on v1

v3 whole, which is shorter than its diff:
```python
import functools
import math

import jax
import jax.numpy as jnp
from jax import lax
from jax.experimental import pallas as pl
from jax.experimental.pallas import tpu as pltpu
from jax.sharding import PartitionSpec as P

HD = 64
ROT = 16
LAYERS = 2
NORM_EPSILON = 1e-05
MASKED = -1e30
F32 = jnp.float32
BF16 = jnp.bfloat16
ROWS = 128
D = 768
HEADS = 3
CTX = 32
TP = 4
RING = 4
GROUPS = CTX // RING
KEYS = RING * ROWS
WIDE = HEADS * HD
QUARTER = ROWS // TP
SCALE = HD**-0.5
QKV = 3 * WIDE
HALF = D // 2
FF_ROWS, AT_ROWS = 2 * D, QKV + WIDE
PHASES = 2 * LAYERS

NN = (((1,), (0,)), ((), ()))
NT = (((1,), (1,)), ((), ()))
TN = (((0,), (0,)), ((), ()))


def dot(a, b, dims=NN):
    return lax.dot_general(a, b, dims, preferred_element_type=F32)


def remote(src, dst, send, recv, ctx=None, tp=None):
    where = {}
    if ctx is not None:
        where["ctx"] = ctx
    if tp is not None:
        where["tp"] = tp
    return pltpu.make_async_remote_copy(
        src_ref=src,
        dst_ref=dst,
        send_sem=send,
        recv_sem=recv,
        device_id=where,
        device_id_type=pl.DeviceIdType.MESH,
    )


def greet(ctx_peers, tp_peers):
    barrier = pltpu.get_barrier_semaphore()
    for peer in ctx_peers:
        pl.semaphore_signal(
            barrier, inc=1, device_id={"ctx": peer}, device_id_type=pl.DeviceIdType.MESH
        )
    for peer in tp_peers:
        pl.semaphore_signal(
            barrier, inc=1, device_id={"tp": peer}, device_id_type=pl.DeviceIdType.MESH
        )
    return barrier, len(ctx_peers) + len(tp_peers)


def centre(residual):
    mean_value = jnp.mean(residual, axis=-1, keepdims=True)
    centred = residual - mean_value
    variance = jnp.mean(centred * centred, axis=-1, keepdims=True)
    inverse = lax.rsqrt(variance + NORM_EPSILON)
    return centred * inverse, inverse


def tp_sum(part, my_tp, phase, s):
    s.tp_mine[...] = part
    s.tp_out[...] = part.astype(BF16)
    slots, gathered = s.tp_slots.at[phase], s.tp_gathered.at[phase]
    send, recv = s.tp_send.at[phase], s.tp_recv.at[phase]

    def quarter(place):
        return pl.ds(pl.multiple_of(place * QUARTER, QUARTER), QUARTER)

    def spread(step):
        peer = lax.rem(my_tp + step, TP)
        return remote(
            s.tp_out.at[quarter(peer)], slots.at[step - 1], send.at[step - 1], recv.at[step - 1], tp=peer
        )

    def collect(step, place):
        return remote(
            gathered.at[quarter(place)],
            gathered.at[quarter(place)],
            send.at[TP - 2 + step],
            recv.at[TP - 2 + step],
            tp=lax.rem(my_tp + step, TP),
        )

    for step in range(1, TP):
        spread(step).start()
    total = s.tp_mine[quarter(my_tp), :]
    for step in range(1, TP):
        spread(step).wait_recv()
        total = total + slots[step - 1].astype(F32)
    gathered[quarter(my_tp), :] = total.astype(BF16)
    for step in range(1, TP):
        collect(step, my_tp).start()
    for step in range(1, TP):
        collect(step, lax.rem(my_tp + TP - step, TP)).wait_recv()
    for step in range(1, TP):
        spread(step).wait_send()
        collect(step, my_tp).wait_send()
    return gathered[...].astype(F32)


RS_MESSAGES, AG_MESSAGES = 6, 6
FLOW_SEMS = 2 * RS_MESSAGES + 1 + 2 * AG_MESSAGES


def rows_at(start, count):
    return pl.ds(pl.multiple_of(start, 16), count)


class Axis:
    def __init__(self, place, of_place):
        self.place = place
        self.of_place = of_place
        self.right = of_place(lax.rem(place + 1, RING))
        self.left = of_place(lax.rem(place + 3, RING))

    def at(self, step):
        return lax.rem(self.place + step + RING, RING)


class ReduceScatter:
    def __init__(self, axis, src, size, cut, first, second, from_left, from_right, sems):
        self.axis, self.src, self.size, self.cut = axis, src, size, cut
        self.first, self.second = first, second
        self.from_left, self.from_right = from_left, from_right
        self.send, self.recv, self.base = sems

    def copy(self, index, src, dst, ctx):
        return remote(
            src, dst, self.send.at[self.base + index], self.recv.at[self.base + index], ctx=ctx
        )

    def copies(self):
        axis, size, cut = self.axis, self.size, self.cut
        rest = size - cut
        far, near_right, near_left = axis.at(2) * size, axis.at(1) * size, axis.at(3) * size
        return [
            self.copy(0, self.src(far, cut), self.first[0].at[pl.ds(0, cut)], axis.right),
            self.copy(1, self.src(far + cut, rest), self.second[0].at[pl.ds(0, rest)], axis.left),
            self.copy(
                2, self.src(near_right + cut, rest), self.from_left.at[pl.ds(cut, rest)], axis.right
            ),
            self.copy(3, self.src(near_left, cut), self.from_right.at[pl.ds(0, cut)], axis.left),
            self.copy(
                4, self.first[1].at[pl.ds(0, cut)], self.from_left.at[pl.ds(0, cut)], axis.right
            ),
            self.copy(
                5, self.second[1].at[pl.ds(0, rest)], self.from_right.at[pl.ds(cut, rest)], axis.left
            ),
        ]

    def start(self):
        for copy in self.copies()[:4]:
            copy.start()

    def middle(self):
        axis, size, cut = self.axis, self.size, self.cut
        rest = size - cut
        copies = self.copies()
        copies[0].wait_recv()
        self.first[1][0:cut, :] = (
            self.first[0][0:cut, :].astype(F32) + self.src(axis.at(1) * size, cut)[...].astype(F32)
        ).astype(BF16)
        copies[4].start()
        copies[1].wait_recv()
        self.second[1][0:rest, :] = (
            self.second[0][0:rest, :].astype(F32)
            + self.src(axis.at(3) * size + cut, rest)[...].astype(F32)
        ).astype(BF16)
        copies[5].start()

    def finish(self, out):
        for copy in self.copies()[2:]:
            copy.wait_recv()
        size = self.size
        out[0:size, :] = (
            self.src(self.axis.place * size, size)[...].astype(F32)
            + self.from_left[0:size, :].astype(F32)
            + self.from_right[0:size, :].astype(F32)
        ).astype(BF16)

    def drain(self):
        for copy in self.copies():
            copy.wait_send()


class AllGather:
    def __init__(self, axis, view, size, cut, sems):
        self.axis, self.view, self.size, self.cut = axis, view, size, cut
        self.send, self.recv, self.base = sems

    def copy(self, index, start, count, ctx):
        part = self.view(start, count)
        return remote(
            part, part, self.send.at[self.base + index], self.recv.at[self.base + index], ctx=ctx
        )

    def copies(self, shift):
        axis, size, cut = self.axis, self.size, self.cut
        rest = size - cut
        if shift == 0:
            own, from_left, from_right = axis.place * size, axis.at(3) * size, axis.at(1) * size
            return [
                self.copy(0, own, cut, axis.right),
                self.copy(1, own + cut, rest, axis.left),
                self.copy(2, own + cut, rest, axis.right),
                self.copy(3, own, cut, axis.left),
                self.copy(4, from_left, cut, axis.right),
                self.copy(5, from_right + cut, rest, axis.left),
            ]
        from_left, from_right, far = axis.at(3) * size, axis.at(1) * size, axis.at(2) * size
        return [
            self.copy(0, from_left, cut, axis.right),
            self.copy(1, from_right + cut, rest, axis.left),
            self.copy(2, from_left + cut, rest, axis.right),
            self.copy(3, from_right, cut, axis.left),
            self.copy(4, far, cut, axis.right),
            self.copy(5, far + cut, rest, axis.left),
        ]

    def start(self):
        for copy in self.copies(0)[:4]:
            copy.start()

    def middle(self):
        come, go = self.copies(1), self.copies(0)
        come[0].wait_recv()
        go[4].start()
        come[1].wait_recv()
        go[5].start()

    def finish(self):
        for copy in self.copies(1)[2:]:
            copy.wait_recv()

    def drain(self):
        for copy in self.copies(0):
            copy.wait_send()


STEPS = 10


def cuts(rows):
    big, sub = rows // RING, rows // RING // RING
    return big // 32 * 16, sub // 32 * 16


def flow_buffers(rows):
    big, sub = rows // RING, rows // RING // RING
    big_cut, sub_cut = cuts(rows)
    counts = [big_cut] * 2 + [big - big_cut] * 2 + [big] * 3
    counts += [sub_cut] * 2 + [sub - sub_cut] * 2 + [sub] * 4
    return [pltpu.VMEM((count, HALF), BF16) for count in counts] + dma_sems(FLOW_SEMS, FLOW_SEMS)


class Flow:
    def __init__(self, axes, across, src_ref, out_ref, half, scratch):
        self.at = 0
        rows = src_ref.shape[0]
        big, sub = rows // RING, rows // RING // RING
        big_cut, sub_cut = cuts(rows)
        one, two = axes
        (a0, a1, b0, b1, left, right, self.big, c0, c1, d0, d1, left2, right2, self.sub, self.other) = (
            scratch[:15]
        )
        self.send, self.recv = scratch[15:]
        lanes = pl.ds(half * HALF, HALF)

        def src(start, count):
            return src_ref.at[rows_at(start, count), lanes]

        def middle_src(start, count):
            return self.big.at[rows_at(start, count)]

        def out(start, count):
            return out_ref.at[rows_at(start, count), lanes]

        corner = one.place * big

        def out_sub(start, count):
            return out_ref.at[rows_at(corner + start, count), lanes]

        self.out_piece = out_sub(two.place * sub, sub)
        self.across = across

        def sems(base):
            return (self.send, self.recv, base)

        self.one = ReduceScatter(one, src, big, big_cut, (a0, a1), (b0, b1), left, right, sems(0))
        self.two = ReduceScatter(
            two, middle_src, sub, sub_cut, (c0, c1), (d0, d1), left2, right2, sems(6)
        )
        self.three = AllGather(two, out_sub, sub, sub_cut, sems(13))
        self.four = AllGather(one, out, big, big_cut, sems(19))

    def swap(self):
        return remote(self.sub, self.other, self.send.at[12], self.recv.at[12], ctx=self.across)

    def advance(self):
        if self.at < STEPS:
            self.step(self.at)
            self.at += 1

    def step(self, number):
        if number == 0:
            self.one.start()
        elif number == 1:
            self.one.middle()
        elif number == 2:
            self.one.finish(self.big)
            self.two.start()
        elif number == 3:
            self.two.middle()
        elif number == 4:
            self.two.finish(self.sub)
            self.swap().start()
        elif number == 5:
            self.swap().wait_recv()
            self.out_piece[...] = (
                self.sub[...].astype(F32) + self.other[...].astype(F32)
            ).astype(BF16)
            self.three.start()
        elif number == 6:
            self.three.middle()
        elif number == 7:
            self.three.finish()
            self.four.start()
        elif number == 8:
            self.four.middle()
        elif number == 9:
            self.four.finish()

    def drain(self):
        self.one.drain()
        self.two.drain()
        self.swap().wait_send()
        self.three.drain()
        self.four.drain()


def dma_sems(*counts):
    return [
        pltpu.SemaphoreType.DMA(count if isinstance(count, tuple) else (count,)) for count in counts
    ]


def scratch():
    sems = dma_sems
    named = dict(
        wq=pltpu.VMEM((LAYERS, QKV, D), BF16),
        wo=pltpu.VMEM((LAYERS, WIDE, D), BF16),
        wu=pltpu.VMEM((LAYERS, D, D), BF16),
        wd=pltpu.VMEM((LAYERS, D, D), BF16),
        resid=pltpu.VMEM((LAYERS, ROWS, D), F32),
        branch=pltpu.VMEM((ROWS, D), F32),
        grad=pltpu.VMEM((ROWS, D), F32),
        norm_part=pltpu.VMEM((ROWS, D), F32),
        pre=pltpu.VMEM((LAYERS, ROWS, D), F32),
        hid=pltpu.VMEM((LAYERS, ROWS, D), BF16),
        kv_t=pltpu.VMEM((LAYERS, 2 * WIDE, KEYS), BF16),
        kv=pltpu.VMEM((LAYERS, KEYS, 2 * WIDE), BF16),
        q=pltpu.VMEM((LAYERS, GROUPS, WIDE, ROWS), BF16),
        att=pltpu.VMEM((LAYERS, WIDE, ROWS), F32),
        lse=pltpu.VMEM((LAYERS, 8, ROWS), F32),
        part_out=pltpu.VMEM((LAYERS, GROUPS, WIDE, ROWS), BF16),
        part_in=pltpu.VMEM((LAYERS, GROUPS, WIDE, ROWS), BF16),
        lse_out=pltpu.VMEM((LAYERS, GROUPS, 8, ROWS), F32),
        lse_in=pltpu.VMEM((LAYERS, GROUPS, 8, ROWS), F32),
        mixed=pltpu.VMEM((LAYERS, GROUPS, WIDE, ROWS), BF16),
        stats=pltpu.VMEM((LAYERS, GROUPS, 8, ROWS), F32),
        query_out=pltpu.VMEM((LAYERS, GROUPS, WIDE, ROWS), BF16),
        query_in=pltpu.VMEM((LAYERS, GROUPS, WIDE, ROWS), BF16),
        pair=pltpu.VMEM((HEADS, 128, 2 * ROWS), BF16),
        terms=pltpu.VMEM((KEYS, 2 * WIDE), F32),
        low_terms=pltpu.VMEM((LAYERS, KEYS, 2 * WIDE), BF16),
        term_slots=pltpu.VMEM((LAYERS, RING - 1, ROWS, 2 * WIDE), BF16),
        query=pltpu.VMEM((WIDE, ROWS), F32),
        merged_t=pltpu.VMEM((QKV, ROWS), BF16),
        ff=pltpu.VMEM((LAYERS, FF_ROWS, D), BF16),
        at=pltpu.VMEM((LAYERS, AT_ROWS, D), BF16),
        tp_mine=pltpu.VMEM((ROWS, D), F32),
        tp_out=pltpu.VMEM((ROWS, D), BF16),
        tp_slots=pltpu.VMEM((PHASES, TP - 1, QUARTER, D), BF16),
        tp_gathered=pltpu.VMEM((PHASES, ROWS, D), BF16),
        small=pltpu.VMEM((4, 16, D), F32),
        small_slots=pltpu.VMEM((4, 4, 16, D), F32),
    )
    for name, shape in dict(
        load=(LAYERS, 4),
        kv_send=(LAYERS, 3),
        kv_recv=(LAYERS, 3),
        term_send=(LAYERS, 3),
        term_recv=(LAYERS, 3),
        tp_send=(PHASES, 2 * TP - 2),
        tp_recv=(PHASES, 2 * TP - 2),
        small_send=(4, 3),
        small_recv=(4, 3),
    ).items():
        named[name] = sems(shape)[0]
    for name in ("q", "part", "lse", "mixed", "stat", "query"):
        named[name + "_go"] = sems((LAYERS, GROUPS))[0]
        named[name + "_come"] = sems((LAYERS, GROUPS))[0]
    return named


class Names:
    def __init__(self, named):
        self.__dict__.update(named)


def rotated(values, rot_ref, sign):
    cosine, sine = rot_ref[0], rot_ref[1] * sign
    rows = []
    for head in range(HEADS):
        start = HD * head
        one, two = values[start : start + 8, :], values[start + 8 : start + 16, :]
        rows.append(one * cosine - two * sine)
        rows.append(two * cosine + one * sine)
        rows.append(values[start + 16 : start + HD, :])
    return jnp.concatenate(rows, axis=0)


def step_kernel(
    x_ref,
    out_grad_ref,
    g1_ref,
    s1_ref,
    g2_ref,
    s2_ref,
    bqkv_ref,
    dense_bias_ref,
    bup_ref,
    down_bias_ref,
    rot_ref,
    wq_hbm,
    wo_hbm,
    wu_hbm,
    wd_hbm,
    out_ref,
    in_grad_ref,
    ff_out,
    at_out,
    g1_out,
    s1_out,
    g2_out,
    s2_out,
    bias_out,
    bqkv_out,
    bup_out,
    *refs,
):
    names = list(scratch())
    s = Names(zip(names, refs))
    flow_refs = refs[len(names) :]
    me = lax.axis_index("ctx")
    my_tp = lax.axis_index("tp")
    z, group = lax.rem(me, RING), me // RING
    weights = ((wq_hbm, s.wq), (wu_hbm, s.wu), (wd_hbm, s.wd), (wo_hbm, s.wo))

    def load(layer, index):
        src, dst = weights[index]
        return pltpu.make_async_copy(src.at[layer], dst.at[layer], s.load.at[layer, index])

    for layer in range(LAYERS):
        for index in range(4):
            load(layer, index).start()
    ring_peers = [group * RING + lax.rem(z + step, RING) for step in range(1, RING)]
    column_peers = [lax.rem(group + step, GROUPS) * RING + z for step in range(1, GROUPS)]
    tp_peers = [lax.rem(my_tp + step, TP) for step in range(1, TP)]
    barrier, greeted = greet(ring_peers + column_peers, tp_peers)

    def vector(ref, layer):
        return ref[...].astype(F32)[layer : layer + 1, :]

    def ring_part(step):
        place = lax.rem(z + step + RING, RING)
        return pl.ds(pl.multiple_of(place * ROWS, ROWS), ROWS)

    def to_group(src, dst, send, recv, target):
        return remote(src, dst, send, recv, ctx=target * RING + z)

    def allowed_pairs():
        key_pos = lax.broadcasted_iota(jnp.int32, (KEYS, ROWS), 0)
        query_pos = z * ROWS + lax.broadcasted_iota(jnp.int32, (KEYS, ROWS), 1)
        return key_pos <= query_pos

    def kv_copy(layer, step, place):
        lanes = ring_part(place)
        return remote(
            s.kv_t.at[layer, :, lanes],
            s.kv_t.at[layer, :, lanes],
            s.kv_send.at[layer, step - 1],
            s.kv_recv.at[layer, step - 1],
            ctx=group * RING + lax.rem(z + step, RING),
        )

    def q_copy(layer, target, source):
        return to_group(
            s.q.at[layer, source],
            s.q.at[layer, source],
            s.q_go.at[layer, target],
            s.q_come.at[layer, source],
            target,
        )

    def part_copies(layer, here, there, target):
        return (
            to_group(
                s.part_out.at[layer, here],
                s.part_in.at[layer, there],
                s.part_go.at[layer, target],
                s.part_come.at[layer, there],
                target,
            ),
            to_group(
                s.lse_out.at[layer, here],
                s.lse_in.at[layer, there],
                s.lse_go.at[layer, target],
                s.lse_come.at[layer, there],
                target,
            ),
        )

    def mixed_copies(layer, entry, target):
        return (
            to_group(
                s.mixed.at[layer, entry],
                s.mixed.at[layer, entry],
                s.mixed_go.at[layer, target],
                s.mixed_come.at[layer, entry],
                target,
            ),
            to_group(
                s.stats.at[layer, entry],
                s.stats.at[layer, entry],
                s.stat_go.at[layer, target],
                s.stat_come.at[layer, entry],
                target,
            ),
        )

    def query_copy(layer, here, there, target):
        return to_group(
            s.query_out.at[layer, here],
            s.query_in.at[layer, there],
            s.query_go.at[layer, target],
            s.query_come.at[layer, there],
            target,
        )

    def term_copy(layer, step):
        return remote(
            s.low_terms.at[layer, ring_part(step)],
            s.term_slots.at[layer, step - 1],
            s.term_send.at[layer, step - 1],
            s.term_recv.at[layer, step - 1],
            ctx=group * RING + lax.rem(z + step, RING),
        )

    def attend(layer, of_query, own):
        for head in range(HEADS):
            rows = slice(HD * head, HD * head + HD)
            keys = s.kv[layer, :, 128 * head : 128 * head + HD]
            scores = dot(keys, s.q[layer, of_query, rows, :]) * SCALE
            if own:
                scores = jnp.where(allowed_pairs(), scores, MASKED)
            highest = jnp.max(scores, axis=0, keepdims=True)
            weights_of = jnp.exp(scores - highest)
            total = jnp.sum(weights_of, axis=0, keepdims=True)
            values_t = s.kv_t[layer, 128 * head + HD : 128 * head + 128, :]
            attended = dot(values_t, weights_of.astype(BF16)) / total
            log_total = highest + jnp.log(total)
            if own:
                s.att[layer, rows, :] = attended
                s.lse[layer, head : head + 1, :] = log_total
            else:
                s.part_out[layer, of_query, rows, :] = attended.astype(BF16)
                s.lse_out[layer, of_query, head : head + 1, :] = log_total

    def forward(layer):
        hat, _ = centre(s.resid[layer])
        normed = (hat * vector(g1_ref, layer) + vector(s1_ref, layer)).astype(BF16)
        load(layer, 0).wait()
        own = ring_part(0)
        for slot in range(3):
            rows = slice(WIDE * slot, WIDE * slot + WIDE)
            bias = bqkv_ref[slot].astype(F32)[layer : layer + 1, :]
            values = (dot(normed, s.wq[layer, rows, :], NT) + bias).T
            if slot < 2:
                values = rotated(values, rot_ref, 1.0)
            values = values.astype(BF16)
            if slot == 0:
                s.q[layer, group] = values
            else:
                for head in range(HEADS):
                    start = 128 * head + HD * (slot - 1)
                    s.kv_t[layer, start : start + HD, own] = values[HD * head : HD * head + HD, :]
        if layer == 0:
            pl.semaphore_wait(barrier, greeted)
        for step in range(1, RING):
            kv_copy(layer, step, 0).start()

        @pl.loop(0, group)
        def _(target):
            q_copy(layer, target, group).start()

        normed = (hat * vector(g2_ref, layer) + vector(s2_ref, layer)).astype(BF16)
        load(layer, 1).wait()
        pre = dot(normed, s.wu[layer]) + vector(bup_ref, layer)
        s.pre[layer] = pre
        hidden = (pre * (1.0 + lax.erf(pre * math.sqrt(0.5))) * 0.5).astype(BF16)
        s.hid[layer] = hidden
        load(layer, 2).wait()
        s.branch[...] = dot(hidden, s.wd[layer])
        for step in range(1, RING):
            kv_copy(layer, step, -step).wait_recv()
        s.kv[layer] = s.kv_t[layer].T
        s.lse[layer] = jnp.zeros((8, ROWS), F32)

        @pl.loop(group + 1, GROUPS)
        def _(of_query):
            q_copy(layer, of_query, of_query).wait_recv()
            s.lse_out[layer, of_query] = jnp.zeros((8, ROWS), F32)
            attend(layer, of_query, False)
            for copy in part_copies(layer, of_query, group, of_query):
                copy.start()

        attend(layer, group, True)

        @pl.loop(0, group)
        def _(source):
            for copy in part_copies(layer, source, source, source):
                copy.wait_recv()
            old, new = s.lse[layer], s.lse_in[layer, source]
            highest = jnp.maximum(old, new)
            old_part, new_part = jnp.exp(old - highest), jnp.exp(new - highest)
            total = old_part + new_part
            s.lse[layer] = highest + jnp.log(total)
            old_part, new_part = old_part / total, new_part / total
            for head in range(HEADS):
                rows = slice(HD * head, HD * head + HD)
                s.att[layer, rows, :] = s.att[layer, rows, :] * old_part[head : head + 1, :] + (
                    s.part_in[layer, source, rows, :].astype(F32) * new_part[head : head + 1, :]
                )

        load(layer, 3).wait()
        branch = s.branch[...] + dot(s.att[layer].astype(BF16), s.wo[layer], TN)
        branch = tp_sum(branch, my_tp, layer, s)
        bias = vector(dense_bias_ref, layer) + vector(down_bias_ref, layer)
        residual = s.resid[layer] + branch + bias
        if layer + 1 < LAYERS:
            s.resid[layer + 1] = residual
        else:
            out_ref[...] = residual.astype(BF16)

    def attend_back(layer, of_query, own):
        for head in range(HEADS):
            rows = slice(HD * head, HD * head + HD)
            lanes = slice(128 * head, 128 * head + 128)
            s.pair[head, :HD, :ROWS] = s.q[layer, of_query, rows, :]
            s.pair[head, HD:, ROWS:] = s.mixed[layer, of_query, rows, :]
            both = dot(s.kv[layer, :, lanes], s.pair[head])
            stats = s.stats[layer, of_query]
            probs = jnp.exp(both[:, :ROWS] * SCALE - stats[head : head + 1, :])
            if own:
                probs = jnp.where(allowed_pairs(), probs, 0.0)
            scores = probs * (both[:, ROWS:] - stats[HEADS + head : HEADS + head + 1, :])
            scores = (scores * SCALE).astype(BF16)
            s.terms[:, lanes] += dot(
                jnp.concatenate([scores, probs.astype(BF16)], axis=1), s.pair[head], NT
            )
            back = dot(s.kv_t[layer, 128 * head : 128 * head + HD, :], scores)
            if own:
                s.query[rows, :] = back
            else:
                s.query_out[layer, of_query, rows, :] = back.astype(BF16)

    def backward(layer, between):
        low = s.grad[...].astype(BF16)
        own_mixed = dot(s.wo[layer], low, NT).astype(BF16)
        s.mixed[layer, group] = own_mixed
        s.stats[layer, group] = jnp.zeros((8, ROWS), F32)
        for head in range(HEADS):
            rows = slice(HD * head, HD * head + HD)
            delta = own_mixed[rows, :].astype(F32) * s.att[layer, rows, :]
            s.stats[layer, group, head : head + 1, :] = s.lse[layer, head : head + 1, :]
            s.stats[layer, group, HEADS + head : HEADS + head + 1, :] = jnp.sum(
                delta, axis=0, keepdims=True
            )

        @pl.loop(0, group)
        def _(target):
            for copy in mixed_copies(layer, group, target):
                copy.start()

        small = s.small.at[0]
        first = 8 * layer
        s.terms[...] = jnp.zeros_like(s.terms)
        small[first + 4 : first + 5, :] = jnp.sum(s.grad[...], axis=0, keepdims=True)
        hat, _ = centre(s.resid[layer])
        gain_one, gain_two = vector(g1_ref, layer), vector(g2_ref, layer)
        hidden_grad = dot(low, s.wd[layer], NT)
        pre = s.pre[layer]
        slope = 0.5 * (1.0 + lax.erf(pre * math.sqrt(0.5))) + pre * jnp.exp(
            -0.5 * pre * pre
        ) * (1.0 / math.sqrt(2.0 * math.pi))
        pre_grad = (hidden_grad * slope).astype(BF16)
        small[first + 6 : first + 7, :] = jnp.sum(pre_grad.astype(F32), axis=0, keepdims=True)
        normed_two = (hat * gain_two + vector(s2_ref, layer)).astype(BF16)
        s.ff[layer, :D, :] = dot(normed_two, pre_grad, TN).astype(BF16)
        s.ff[layer, D:, :] = dot(s.hid[layer], low, TN).astype(BF16)
        between(0)
        grad_two = dot(pre_grad, s.wu[layer], NT)
        small[first + 2 : first + 3, :] = jnp.sum(grad_two * hat, axis=0, keepdims=True)
        small[first + 3 : first + 4, :] = jnp.sum(grad_two, axis=0, keepdims=True)
        s.norm_part[...] = grad_two * gain_two

        @pl.loop(group + 1, GROUPS)
        def _(of_query):
            for copy in mixed_copies(layer, of_query, of_query):
                copy.wait_recv()
            attend_back(layer, of_query, False)
            query_copy(layer, of_query, group, of_query).start()

        attend_back(layer, group, True)
        s.low_terms[layer] = s.terms[...].astype(BF16)
        for step in range(1, RING):
            term_copy(layer, step).start()
        s.at[layer, QKV:, :] = dot(s.att[layer].astype(BF16), s.grad[...].astype(BF16)).astype(BF16)
        between(1)

        keys_values = s.terms[ring_part(0), :]
        for step in range(1, RING):
            term_copy(layer, step).wait_recv()
            keys_values = keys_values + s.term_slots[layer, step - 1].astype(F32)

        @pl.loop(0, group)
        def _(source):
            query_copy(layer, source, source, source).wait_recv()
            s.query[...] += s.query_in[layer, source].astype(F32)

        across = keys_values.T
        keys = jnp.concatenate(
            [across[128 * head : 128 * head + HD, :] for head in range(HEADS)], axis=0
        )
        s.merged_t[:WIDE, :] = rotated(s.query[...], rot_ref, -1.0).astype(BF16)
        s.merged_t[WIDE : 2 * WIDE, :] = rotated(keys, rot_ref, -1.0).astype(BF16)
        for head in range(HEADS):
            start = 2 * WIDE + HD * head
            s.merged_t[start : start + HD, :] = across[
                128 * head + HD : 128 * head + 128, :
            ].astype(BF16)
        merged = s.merged_t[...].T
        grad_one = dot(merged, s.wq[layer])
        hat, inverse = centre(s.resid[layer])

        def attention_weights():
            normed_one = (hat * gain_one + vector(s1_ref, layer)).astype(BF16)
            s.at[layer, :QKV, :] = dot(s.merged_t[...], normed_one).astype(BF16)
            between(2)

        if layer == 0:
            attention_weights()
        small[first : first + 1, :] = jnp.sum(grad_one * hat, axis=0, keepdims=True)
        small[first + 1 : first + 2, :] = jnp.sum(grad_one, axis=0, keepdims=True)
        small[first + 5 : first + 6, :] = jnp.zeros((1, D), F32)
        small[first + 5 : first + 6, :QKV] = jnp.sum(merged.astype(F32), axis=0, keepdims=True)
        small[first + 7 : first + 8, :] = jnp.zeros((1, D), F32)
        total = tp_sum(s.norm_part[...] + grad_one * gain_one, my_tp, LAYERS + layer, s)
        along = jnp.mean(total * hat, axis=-1, keepdims=True)
        level = jnp.mean(total, axis=-1, keepdims=True)
        grad = s.grad[...] + inverse * (total - level - hat * along)
        if layer > 0:
            s.grad[...] = grad
            attention_weights()
        else:
            in_grad_ref[...] = grad

    x, y = lax.rem(me // 4, 2), me // 8
    opposite = me + 4 - 8 * x
    z_axis = Axis(z, lambda place: me - z + place)
    y_axis = Axis(y, lambda place: me + (place - y) * 8)
    flows = {}
    per = len(flow_buffers(FF_ROWS))
    for layer in range(LAYERS):
        for kind, src, out in (("ff", s.ff, ff_out), ("at", s.at, at_out)):
            made = []
            for half in range(2):
                axes = (z_axis, y_axis) if half == 0 else (y_axis, z_axis)
                mine, flow_refs = flow_refs[:per], flow_refs[per:]
                made.append(Flow(axes, opposite, src.at[layer], out.at[layer], half, mine))
            flows[kind, layer] = made

    def advance(*which):
        for key in which:
            for one in flows[key]:
                one.advance()

    def between_last(point):
        if point == 0:
            advance(("ff", 1))
        elif point == 1:
            advance(("ff", 1))
        else:
            advance(("ff", 1), ("at", 1))

    def between_first(point):
        if point == 0:
            advance(("ff", 1), ("at", 1), ("ff", 0))
        elif point == 1:
            advance(("ff", 1), ("at", 1), ("ff", 0))
        else:
            advance(("at", 0), ("ff", 1), ("at", 1), ("ff", 0))

    s.resid[0] = x_ref[...].astype(F32)
    s.pair[...] = jnp.zeros_like(s.pair)
    for layer in range(LAYERS):
        forward(layer)
    s.grad[...] = out_grad_ref[...].astype(F32)
    backward(1, between_last)
    backward(0, between_first)

    z_peers = [z_axis.of_place(z_axis.at(step)) for step in (1, 2, 3)]
    y_peers = [y_axis.of_place(y_axis.at(step)) for step in (1, 2, 3)]
    stage_peers = (z_peers, y_peers, [opposite], tp_peers)
    places = (z, y, x, my_tp)

    def small_copies(stage):
        return [
            remote(
                s.small.at[stage],
                s.small_slots.at[stage, places[stage]],
                s.small_send.at[stage, step],
                s.small_recv.at[stage, step],
                **({"tp": peer} if stage == 3 else {"ctx": peer}),
            )
            for step, peer in enumerate(stage_peers[stage])
        ]

    def small_total(stage):
        for copy in small_copies(stage):
            copy.wait_recv()
        s.small_slots[stage, places[stage]] = s.small[stage]
        total = s.small_slots[stage, 0]
        for place in range(1, 2 if stage == 2 else 4):
            total = total + s.small_slots[stage, place]
        return total

    def small_step(number):
        if 0 < number < 4:
            s.small[number] = small_total(number - 1)
        if number < 4:
            for copy in small_copies(number):
                copy.start()
        elif number == 4:
            total, part = small_total(3), s.small[3]
            for row, ref in enumerate((g1_out, s1_out, g2_out, s2_out)):
                for layer in range(LAYERS):
                    ref[layer : layer + 1, :] = total[8 * layer + row : 8 * layer + row + 1, :]
            for layer in range(LAYERS):
                bias_out[layer : layer + 1, :] = part[8 * layer + 4 : 8 * layer + 5, :]
                bup_out[layer : layer + 1, :] = part[8 * layer + 6 : 8 * layer + 7, :]
                for slot in range(3):
                    bqkv_out[slot, layer : layer + 1, :] = part[
                        8 * layer + 5 : 8 * layer + 6, WIDE * slot : WIDE * slot + WIDE
                    ]

    order = (("ff", 1), ("at", 1), ("ff", 0), ("at", 0))
    for number in range(STEPS):
        small_step(number)
        advance(*order)

    for layer in range(LAYERS):
        for step in range(1, RING):
            kv_copy(layer, step, 0).wait_send()
            term_copy(layer, step).wait_send()

        @pl.loop(0, group)
        def _(target):
            q_copy(layer, target, group).wait_send()
            for copy in mixed_copies(layer, group, target):
                copy.wait_send()

        @pl.loop(group + 1, GROUPS)
        def _(of_query):
            query_copy(layer, of_query, group, of_query).wait_send()
            for copy in part_copies(layer, of_query, group, of_query):
                copy.wait_send()

    for key in order:
        for one in flows[key]:
            one.drain()
    for stage in range(4):
        for copy in small_copies(stage):
            copy.wait_send()


def vmem(count):
    return [pl.BlockSpec(memory_space=pltpu.VMEM)] * count


def hbm(count):
    return [pl.BlockSpec(memory_space=pl.ANY)] * count


def whole_step(*arrays):
    pair = jax.ShapeDtypeStruct((LAYERS, D), F32)
    buffers = []
    for _ in range(LAYERS):
        for rows in (FF_ROWS, AT_ROWS):
            buffers += flow_buffers(rows) * 2
    return pl.pallas_call(
        step_kernel,
        name="training_step",
        out_shape=[
            jax.ShapeDtypeStruct((ROWS, D), BF16),
            jax.ShapeDtypeStruct((ROWS, D), F32),
            jax.ShapeDtypeStruct((LAYERS, FF_ROWS, D), BF16),
            jax.ShapeDtypeStruct((LAYERS, AT_ROWS, D), BF16),
            pair,
            pair,
            pair,
            pair,
            pair,
            jax.ShapeDtypeStruct((3, LAYERS, WIDE), F32),
            pair,
        ],
        in_specs=vmem(11) + hbm(4),
        out_specs=vmem(11),
        scratch_shapes=[*scratch().values(), *buffers],
        compiler_params=pltpu.CompilerParams(
            collective_id=0, has_side_effects=True, vmem_limit_bytes=60 << 20
        ),
    )(*arrays)


def on_device(
    layer_input,
    attention_gain,
    attention_shift,
    feedforward_gain,
    feedforward_shift,
    query_key_value_weight,
    query_key_value_bias,
    attention_out_weight,
    dense_bias,
    expand_weight,
    expand_bias,
    down_weight,
    down_bias,
    output_grad,
):
    me = lax.axis_index("ctx")
    positions = (me * ROWS + jnp.arange(ROWS, dtype=jnp.int32)).astype(F32)
    inverse = jnp.power(10000.0, -2.0 * jnp.arange(ROT // 2, dtype=F32) / ROT)
    angles = inverse[:, None] * positions[None, :]
    rot = jnp.stack([jnp.cos(angles), jnp.sin(angles)])
    output, grad, ff, at, g1, s1, g2, s2, bias, bqkv, bup = whole_step(
        layer_input[0],
        output_grad[0],
        attention_gain,
        attention_shift,
        feedforward_gain,
        feedforward_shift,
        query_key_value_bias.transpose(1, 0, 2),
        dense_bias,
        expand_bias,
        down_bias,
        rot,
        query_key_value_weight.transpose(0, 2, 3, 1).reshape(LAYERS, QKV, D),
        attention_out_weight,
        expand_weight,
        down_weight,
    )
    return (
        output[None],
        grad[None],
        g1,
        s1,
        g2,
        s2,
        at[:, :QKV].astype(F32).reshape(LAYERS, 3, WIDE, D).transpose(0, 3, 1, 2),
        bqkv.transpose(1, 0, 2),
        at[:, QKV:].astype(F32),
        bias,
        ff[:, :D].astype(F32),
        bup,
        ff[:, D:].astype(F32),
        bias,
    )


def solution(mesh):
    in_specs = (
        P(None, "ctx", None),
        P(),
        P(),
        P(),
        P(),
        P(None, None, None, "tp"),
        P(None, None, "tp"),
        P(None, "tp", None),
        P(),
        P(None, None, "tp"),
        P(None, "tp"),
        P(None, "tp", None),
        P(),
        P(None, "ctx", None),
    )
    out_specs = (
        P(None, "ctx", None),
        P(None, "ctx", None),
        P(),
        P(),
        P(),
        P(),
        P(None, None, None, "tp"),
        P(None, None, "tp"),
        P(None, "tp", None),
        P(),
        P(None, None, "tp"),
        P(None, "tp"),
        P(None, "tp", None),
        P(),
    )
    return jax.shard_map(
        on_device, mesh=mesh, in_specs=in_specs, out_specs=out_specs, check_vma=False
    )
```

time: 451 us -> 194 us (0.43)
  Pallas kernels: 400 us -> 176 us
  local copies, waits for them, and re-layouts: 31.5 us -> 6.32 us
  other arithmetic: 17.3 us -> 11 us
    pallas_call x5 -> x1, Pallas kernels: 400 us -> 176 us  [whole_step(): pl.pallas_call(step_kernel, name='training_step', out_shape=[jax.ShapeDty...]
    another operation x22 -> x0, local copies, waits for them, and re-layouts: 12.3 us -> none  [the longest x4 4.64 us: part(): jnp.stack([total[start:start + count] for total in totals]).astype(F32)]
    reshape x9 -> x0, local copies, waits for them, and re-layouts: 5.3 us -> none  [the longest x2 1.5 us: packed_qkv(): pairs.reshape(*lead, 2 * HEADS * HD)]
    slice x6 -> x1, local copies, waits for them, and re-layouts: 4.85 us -> 0.11 us  [on_device(): at[:, :QKV].astype(F32).reshape(LAYERS, 3, WIDE, D).transpose(0, 3, 1, 2)]
    convert_element_type x6 -> x2, other arithmetic: 11 us -> 8.18 us  [the longest x1 7.09 us: on_device(): ff[:, D:].astype(F32)]
where the time goes in v3:
time: 194 us
  Pallas kernels  176 us (91%)
  other arithmetic  11 us (6%)
  local copies, waits for them, and re-layouts  6.32 us (3%)
    pallas_call x1, Pallas kernels, whole_step(): pl.pallas_call(step_kernel, name='training_step', out_shape=[jax.ShapeDty...  176 us
    convert_element_type x1, other arithmetic, on_device(): ff[:, D:].astype(F32)  7.09 us
    unnamed x30, local copies, waits for them, and re-layouts  6.21 us

profile of v3, /device:TPU:0, one launch (start us, length us, event | category | flops | bytes accessed | tf_op | source)
XLA Modules:
  0.0 194.2 jit_solution(1224806210221904609)
XLA Ops:
  0.7 0.1 multiply_cosine_fusion
  0.8 0.6 pad_maximum_fusion.rot_ref
  1.4 176.1 %training_step.1 = (bf16[128,768]{1,0:T(8,128)(2,1)}, f32[128,768]{1,0:T(8,128)}, bf16[2,1536,768]{2,1,0:T(8,128)(2,1)}, bf16[2,768,768]{2,1,0:T(8,128)(2,1)}, f...) custom-call(bf16[128,768]{1,0:T(8,128)(2,1)} %bitcast.17, ...), custom_call_target="tpu_custom_call" | custom-call | tf_op jit(solution)/shard_map/training_step/pallas_call | solution.py:932
  177.5 0.0 copy-start
  177.5 7.1 %slice_convert_fusion = (f32[2,768,768]{2,1,0:T(8,128)}, f32[2,768,768]{2,1,0:T(8,128)}) fusion(bf16[2,1536,768]{2,1,0:T(8,128)(2,1)} %get-tuple-element.34), kind=kLoop, calls=%fused_computation.1 | loop fusion | flops 2359296 | bytes 14155776 | tf_op jit(solution)/shard_map/convert_element_type | solution.py:1008
  184.6 0.0 copy-done
  184.6 0.1 slice.12
  184.7 0.0 copy-start.3
  184.8 0.0 copy-start.2
  184.8 2.1 %convert_bitcast_fusion = f32[2,768,3,192]{1,3,2,0:T(8,128)} fusion(bf16[2,3,192,768]{3,2,1,0:T(8,128)(2,1)S(1)} %bitcast.13), kind=kLoop, calls=%fused_computation | loop fusion | flops 884736 | bytes 5308416 | tf_op jit(solution)/shard_map/transpose | solution.py:1002
  186.9 0.0 copy-start.6
  186.9 0.0 copy-start.5
  186.9 1.1 slice_convert_fusion.2
  188.0 0.6 copy.38
  188.6 0.7 copy.39
  189.3 0.7 copy.40
  190.0 0.6 copy.41
  190.6 0.6 copy.42
  191.2 0.6 copy.43
  191.8 0.0 copy-done.6
  191.8 0.6 copy.44
  192.4 0.6 copy.45
  193.0 0.6 copy.46
  193.6 0.6 copy.47
  (15 shorter events, 0.0 us)
Async XLA Ops:
  177.5 7.1 %copy-start = (bf16[2,768,768]{2,1,0:T(8,128)(2,1)S(1)}, bf16[2,768,768]{2,1,0:T(8,128)(2,1)}, u32[]{:S(2)}) copy-start(bf16[2,768,768]{2,1,0:T(8,128)(2,1)} %get-tuple-element.31) | copy-start | bytes 7077892
  184.7 3.3 %copy-start.3 = (f32[2,768]{1,0:T(2,128)S(1)}, f32[2,768]{1,0:T(2,128)}, u32[]{:S(2)}) copy-start(f32[2,768]{1,0:T(2,128)} %get-tuple-element.91) | copy-start | bytes 18436
  184.8 3.9 %copy-start.2 = (bf16[128,768]{1,0:T(8,128)(2,1)S(1)}, bf16[128,768]{1,0:T(8,128)(2,1)}, u32[]{:S(2)}) copy-start(bf16[128,768]{1,0:T(8,128)(2,1)} %get-tuple-element.25) | copy-start | bytes 589828
  186.9 2.4 %copy-start.1 = (f32[128,768]{1,0:T(8,128)S(1)}, f32[128,768]{1,0:T(8,128)}, u32[]{:S(2)}) copy-start(f32[128,768]{1,0:T(8,128)} %get-tuple-element.26) | copy-start | bytes 1179652
  186.9 3.2 %copy-start.9 = (f32[2,768]{1,0:T(2,128)S(1)}, f32[2,768]{1,0:T(2,128)}, u32[]{:S(2)}) copy-start(f32[2,768]{1,0:T(2,128)} %get-tuple-element.84) | copy-start | bytes 18436
  186.9 3.8 %copy-start.8 = (f32[2,768]{1,0:T(2,128)S(1)}, f32[2,768]{1,0:T(2,128)}, u32[]{:S(2)}) copy-start(f32[2,768]{1,0:T(2,128)} %get-tuple-element.85) | copy-start | bytes 18436
  186.9 4.3 %copy-start.7 = (f32[2,768]{1,0:T(2,128)S(1)}, f32[2,768]{1,0:T(2,128)}, u32[]{:S(2)}) copy-start(f32[2,768]{1,0:T(2,128)} %get-tuple-element.86) | copy-start | bytes 18436
  186.9 4.9 %copy-start.6 = (f32[2,768]{1,0:T(2,128)S(1)}, f32[2,768]{1,0:T(2,128)}, u32[]{:S(2)}) copy-start(f32[2,768]{1,0:T(2,128)} %get-tuple-element.87) | copy-start | bytes 18436
  186.9 5.5 %copy-start.5 = (f32[3,2,192]{2,1,0:T(2,128)S(1)}, f32[3,2,192]{2,1,0:T(2,128)}, u32[]{:S(2)}) copy-start(f32[3,2,192]{2,1,0:T(2,128)} %get-tuple-element.32) | copy-start | bytes 13828
  186.9 6.7 %copy-start.4 = (f32[2,768]{1,0:T(2,128)S(1)}, f32[2,768]{1,0:T(2,128)}, u32[]{:S(2)}) copy-start(f32[2,768]{1,0:T(2,128)} %get-tuple-element.93) | copy-start | bytes 18436

commit v4 on v3

--- a/solution.py
+++ b/solution.py
@@ -77,7 +77,7 @@
     return centred * inverse, inverse
 
 
-def tp_sum(part, my_tp, phase, s):
+def tp_sum(part, my_tp, phase, s, between=lambda point: None):
     s.tp_mine[...] = part
     s.tp_out[...] = part.astype(BF16)
     slots, gathered = s.tp_slots.at[phase], s.tp_gathered.at[phase]
@@ -103,6 +103,7 @@
 
     for step in range(1, TP):
         spread(step).start()
+    between(6)
     total = s.tp_mine[quarter(my_tp), :]
     for step in range(1, TP):
         spread(step).wait_recv()
@@ -110,6 +111,7 @@
     gathered[quarter(my_tp), :] = total.astype(BF16)
     for step in range(1, TP):
         collect(step, my_tp).start()
+    between(7)
     for step in range(1, TP):
         collect(step, lax.rem(my_tp + TP - step, TP)).wait_recv()
     for step in range(1, TP):
@@ -268,8 +270,8 @@
 def flow_buffers(rows):
     big, sub = rows // RING, rows // RING // RING
     big_cut, sub_cut = cuts(rows)
-    counts = [big_cut] * 2 + [big - big_cut] * 2 + [big] * 3
-    counts += [sub_cut] * 2 + [sub - sub_cut] * 2 + [sub] * 4
+    counts = [big_cut, big - big_cut, big, big]
+    counts += [sub_cut, sub - sub_cut, sub, sub, sub]
     return [pltpu.VMEM((count, HALF), BF16) for count in counts] + dma_sems(FLOW_SEMS, FLOW_SEMS)
 
 
@@ -280,10 +282,9 @@
         big, sub = rows // RING, rows // RING // RING
         big_cut, sub_cut = cuts(rows)
         one, two = axes
-        (a0, a1, b0, b1, left, right, self.big, c0, c1, d0, d1, left2, right2, self.sub, self.other) = (
-            scratch[:15]
-        )
-        self.send, self.recv = scratch[15:]
+        a, b, left, right, c, d, left2, right2, self.other = scratch[:9]
+        self.big, self.sub = left, left2
+        self.send, self.recv = scratch[9:]
         lanes = pl.ds(half * HALF, HALF)
 
         def src(start, count):
@@ -306,9 +307,9 @@
         def sems(base):
             return (self.send, self.recv, base)
 
-        self.one = ReduceScatter(one, src, big, big_cut, (a0, a1), (b0, b1), left, right, sems(0))
+        self.one = ReduceScatter(one, src, big, big_cut, (a, a), (b, b), left, right, sems(0))
         self.two = ReduceScatter(
-            two, middle_src, sub, sub_cut, (c0, c1), (d0, d1), left2, right2, sems(6)
+            two, middle_src, sub, sub_cut, (c, c), (d, d), left2, right2, sems(6)
         )
         self.three = AllGather(two, out_sub, sub, sub_cut, sems(13))
         self.four = AllGather(one, out, big, big_cut, sems(19))
@@ -374,7 +375,6 @@
         resid=pltpu.VMEM((LAYERS, ROWS, D), F32),
         branch=pltpu.VMEM((ROWS, D), F32),
         grad=pltpu.VMEM((ROWS, D), F32),
-        norm_part=pltpu.VMEM((ROWS, D), F32),
         pre=pltpu.VMEM((LAYERS, ROWS, D), F32),
         hid=pltpu.VMEM((LAYERS, ROWS, D), BF16),
         kv_t=pltpu.VMEM((LAYERS, 2 * WIDE, KEYS), BF16),
@@ -440,6 +440,10 @@
     return jnp.concatenate(rows, axis=0)
 
 
+FF1, AT1, FF0, AT0 = ("ff", 1), ("at", 1), ("ff", 0), ("at", 0)
+PLAN = {1: {1: (FF1,), 4: (FF1,), 7: (FF1,), 8: (AT1,)}, 0: {0: (FF1,), 1: (AT1, FF0), 4: (FF1, AT1, FF0), 5: (AT0,), 7: (FF1, AT1, FF0)}}
+
+
 def step_kernel(
     x_ref,
     out_grad_ref,
@@ -460,13 +464,8 @@
     in_grad_ref,
     ff_out,
     at_out,
-    g1_out,
-    s1_out,
-    g2_out,
-    s2_out,
-    bias_out,
+    small_out,
     bqkv_out,
-    bup_out,
     *refs,
 ):
     names = list(scratch())
@@ -713,6 +712,7 @@
             for copy in mixed_copies(layer, group, target):
                 copy.start()
 
+        between(0)
         small = s.small.at[0]
         first = 8 * layer
         s.terms[...] = jnp.zeros_like(s.terms)
@@ -729,11 +729,12 @@
         normed_two = (hat * gain_two + vector(s2_ref, layer)).astype(BF16)
         s.ff[layer, :D, :] = dot(normed_two, pre_grad, TN).astype(BF16)
         s.ff[layer, D:, :] = dot(s.hid[layer], low, TN).astype(BF16)
-        between(0)
+        between(1)
         grad_two = dot(pre_grad, s.wu[layer], NT)
         small[first + 2 : first + 3, :] = jnp.sum(grad_two * hat, axis=0, keepdims=True)
         small[first + 3 : first + 4, :] = jnp.sum(grad_two, axis=0, keepdims=True)
-        s.norm_part[...] = grad_two * gain_two
+        s.branch[...] = grad_two * gain_two
+        between(2)
 
         @pl.loop(group + 1, GROUPS)
         def _(of_query):
@@ -742,12 +743,13 @@
             attend_back(layer, of_query, False)
             query_copy(layer, of_query, group, of_query).start()
 
+        between(3)
         attend_back(layer, group, True)
         s.low_terms[layer] = s.terms[...].astype(BF16)
         for step in range(1, RING):
             term_copy(layer, step).start()
         s.at[layer, QKV:, :] = dot(s.att[layer].astype(BF16), s.grad[...].astype(BF16)).astype(BF16)
-        between(1)
+        between(4)
 
         keys_values = s.terms[ring_part(0), :]
         for step in range(1, RING):
@@ -777,16 +779,16 @@
         def attention_weights():
             normed_one = (hat * gain_one + vector(s1_ref, layer)).astype(BF16)
             s.at[layer, :QKV, :] = dot(s.merged_t[...], normed_one).astype(BF16)
-            between(2)
 
         if layer == 0:
             attention_weights()
+        between(5)
         small[first : first + 1, :] = jnp.sum(grad_one * hat, axis=0, keepdims=True)
         small[first + 1 : first + 2, :] = jnp.sum(grad_one, axis=0, keepdims=True)
         small[first + 5 : first + 6, :] = jnp.zeros((1, D), F32)
         small[first + 5 : first + 6, :QKV] = jnp.sum(merged.astype(F32), axis=0, keepdims=True)
         small[first + 7 : first + 8, :] = jnp.zeros((1, D), F32)
-        total = tp_sum(s.norm_part[...] + grad_one * gain_one, my_tp, LAYERS + layer, s)
+        total = tp_sum(s.branch[...] + grad_one * gain_one, my_tp, LAYERS + layer, s, between)
         along = jnp.mean(total * hat, axis=-1, keepdims=True)
         level = jnp.mean(total, axis=-1, keepdims=True)
         grad = s.grad[...] + inverse * (total - level - hat * along)
@@ -795,6 +797,7 @@
             attention_weights()
         else:
             in_grad_ref[...] = grad
+        between(8)
 
     x, y = lax.rem(me // 4, 2), me // 8
     opposite = me + 4 - 8 * x
@@ -816,29 +819,16 @@
             for one in flows[key]:
                 one.advance()
 
-    def between_last(point):
-        if point == 0:
-            advance(("ff", 1))
-        elif point == 1:
-            advance(("ff", 1))
-        else:
-            advance(("ff", 1), ("at", 1))
-
-    def between_first(point):
-        if point == 0:
-            advance(("ff", 1), ("at", 1), ("ff", 0))
-        elif point == 1:
-            advance(("ff", 1), ("at", 1), ("ff", 0))
-        else:
-            advance(("at", 0), ("ff", 1), ("at", 1), ("ff", 0))
+    def between(layer):
+        return lambda point: advance(*PLAN[layer].get(point, ()))
 
     s.resid[0] = x_ref[...].astype(F32)
     s.pair[...] = jnp.zeros_like(s.pair)
     for layer in range(LAYERS):
         forward(layer)
     s.grad[...] = out_grad_ref[...].astype(F32)
-    backward(1, between_last)
-    backward(0, between_first)
+    backward(1, between(1))
+    backward(0, between(0))
 
     z_peers = [z_axis.of_place(z_axis.at(step)) for step in (1, 2, 3)]
     y_peers = [y_axis.of_place(y_axis.at(step)) for step in (1, 2, 3)]
@@ -874,18 +864,19 @@
                 copy.start()
         elif number == 4:
             total, part = small_total(3), s.small[3]
-            for row, ref in enumerate((g1_out, s1_out, g2_out, s2_out)):
-                for layer in range(LAYERS):
-                    ref[layer : layer + 1, :] = total[8 * layer + row : 8 * layer + row + 1, :]
             for layer in range(LAYERS):
-                bias_out[layer : layer + 1, :] = part[8 * layer + 4 : 8 * layer + 5, :]
-                bup_out[layer : layer + 1, :] = part[8 * layer + 6 : 8 * layer + 7, :]
+                for row in range(4):
+                    small_out[row, layer : layer + 1, :] = total[8 * layer + row : 8 * layer + row + 1, :]
+                for row in (4, 6):
+                    small_out[row, layer : layer + 1, :] = part[8 * layer + row : 8 * layer + row + 1, :]
+                for row in (5, 7):
+                    small_out[row, layer : layer + 1, :] = jnp.zeros((1, D), F32)
                 for slot in range(3):
                     bqkv_out[slot, layer : layer + 1, :] = part[
                         8 * layer + 5 : 8 * layer + 6, WIDE * slot : WIDE * slot + WIDE
                     ]
 
-    order = (("ff", 1), ("at", 1), ("ff", 0), ("at", 0))
+    order = (AT0, FF0, AT1, FF1)
     for number in range(STEPS):
         small_step(number)
         advance(*order)
@@ -924,7 +915,6 @@
 
 
 def whole_step(*arrays):
-    pair = jax.ShapeDtypeStruct((LAYERS, D), F32)
     buffers = []
     for _ in range(LAYERS):
         for rows in (FF_ROWS, AT_ROWS):
@@ -937,16 +927,11 @@
             jax.ShapeDtypeStruct((ROWS, D), F32),
             jax.ShapeDtypeStruct((LAYERS, FF_ROWS, D), BF16),
             jax.ShapeDtypeStruct((LAYERS, AT_ROWS, D), BF16),
-            pair,
-            pair,
-            pair,
-            pair,
-            pair,
+            jax.ShapeDtypeStruct((8, LAYERS, D), F32),
             jax.ShapeDtypeStruct((3, LAYERS, WIDE), F32),
-            pair,
         ],
         in_specs=vmem(11) + hbm(4),
-        out_specs=vmem(11),
+        out_specs=vmem(6),
         scratch_shapes=[*scratch().values(), *buffers],
         compiler_params=pltpu.CompilerParams(
             collective_id=0, has_side_effects=True, vmem_limit_bytes=60 << 20
@@ -975,7 +960,7 @@
     inverse = jnp.power(10000.0, -2.0 * jnp.arange(ROT // 2, dtype=F32) / ROT)
     angles = inverse[:, None] * positions[None, :]
     rot = jnp.stack([jnp.cos(angles), jnp.sin(angles)])
-    output, grad, ff, at, g1, s1, g2, s2, bias, bqkv, bup = whole_step(
+    output, grad, ff, at, small, bqkv = whole_step(
         layer_input[0],
         output_grad[0],
         attention_gain,
@@ -995,18 +980,18 @@
     return (
         output[None],
         grad[None],
-        g1,
-        s1,
-        g2,
-        s2,
+        small[0],
+        small[1],
+        small[2],
+        small[3],
         at[:, :QKV].astype(F32).reshape(LAYERS, 3, WIDE, D).transpose(0, 3, 1, 2),
         bqkv.transpose(1, 0, 2),
         at[:, QKV:].astype(F32),
-        bias,
+        small[4],
         ff[:, :D].astype(F32),
-        bup,
+        small[6],
         ff[:, D:].astype(F32),
-        bias,
+        small[4],
     )
 
 

time: 194 us -> 184 us (0.948)
  Pallas kernels: 176 us -> 168 us
  local copies, waits for them, and re-layouts: 6.32 us -> 4.13 us
    pallas_call x1, Pallas kernels: 176 us -> 168 us  [whole_step(): pl.pallas_call(step_kernel, name='training_step', out_shape=[jax.ShapeDty...]
    unnamed x30 -> x14, local copies, waits for them, and re-layouts: 6.21 us -> 2.63 us
where the time goes in v4:
time: 184 us; the launch traced here: 183 us
  Pallas kernels  168 us (91%)
  other arithmetic  11 us (6%)
  local copies, waits for them, and re-layouts  4.13 us (2%)
    pallas_call x1, Pallas kernels, whole_step(): pl.pallas_call(step_kernel, name='training_step', out_shape=[jax.ShapeDty...  168 us
    convert_element_type x1, other arithmetic, on_device(): ff[:, D:].astype(F32)  7.09 us

profile of v4, /device:TPU:0, one launch (start us, length us, event | category | flops | bytes accessed | tf_op | source)
XLA Modules:
  0.0 183.4 jit_solution(15388898956723583106)
XLA Ops:
  0.7 0.1 multiply_cosine_fusion
  0.8 0.6 pad_maximum_fusion.rot_ref
  1.4 167.5 %training_step.1 = (bf16[128,768]{1,0:T(8,128)(2,1)}, f32[128,768]{1,0:T(8,128)}, bf16[2,1536,768]{2,1,0:T(8,128)(2,1)}, bf16[2,768,768]{2,1,0:T(8,128)(2,1)}, f...) custom-call(bf16[128,768]{1,0:T(8,128)(2,1)} %bitcast.29, bf16[128,768]{1,0:T(8,128)(2,1)} %bitcast.30, bf16[2,768]{1,0:T(2,128)(2,1)} %g1_ref.1, ...), custom_call_target="tpu_custom_call" | custom-call | tf_op jit(solution)/shard_map/training_step/pallas_call | solution.py:922
  169.0 1.4 slice_bitcast_fusion
  170.3 0.0 copy-start.3
  170.3 0.0 copy-start
  170.3 7.1 %slice_convert_fusion = (f32[2,768,768]{2,1,0:T(8,128)}, f32[2,768,768]{2,1,0:T(8,128)}) fusion(bf16[2,1536,768]{2,1,0:T(8,128)(2,1)} %get-tuple-element.25), kind=kLoop, calls=%fused_computation.1 | loop fusion | flops 2359296 | bytes 14155776 | tf_op jit(solution)/shard_map/convert_element_type | solution.py:993
  177.4 0.0 copy-done
  177.4 0.1 slice.35
  177.6 0.0 copy-start.2
  177.6 2.1 %convert_bitcast_fusion = f32[2,768,3,192]{1,3,2,0:T(8,128)} fusion(bf16[2,3,192,768]{3,2,1,0:T(8,128)(2,1)S(1)} %bitcast.25), kind=kLoop, calls=%fused_computation | loop fusion | flops 884736 | bytes 5308416 | tf_op jit(solution)/shard_map/transpose | solution.py:987
  179.7 0.0 copy-start.1
  179.7 0.0 copy-start.4
  179.7 1.1 slice_convert_fusion.2
  180.8 0.0 copy-done.3
  180.8 0.6 copy.32
  181.4 0.0 copy-done.2
  181.4 0.7 copy.33
  182.0 0.0 copy-done.1
  182.1 0.7 copy.34
  182.8 0.0 copy-done.4
  182.8 0.6 copy.35
  (2 shorter events, 0.0 us)
Async XLA Ops:
  170.3 10.4 %copy-start.3 = (f32[2,768]{1,0:T(2,128)}, f32[2,768]{1,0:T(2,128)S(1)}, u32[]{:S(2)}) copy-start(f32[2,768]{1,0:T(2,128)S(1)} %get-tuple-element.87) | copy-start | bytes 18436
  170.3 7.1 %copy-start = (bf16[2,768,768]{2,1,0:T(8,128)(2,1)S(1)}, bf16[2,768,768]{2,1,0:T(8,128)(2,1)}, u32[]{:S(2)}) copy-start(bf16[2,768,768]{2,1,0:T(8,128)(2,1)} %get-tuple-element.23) | copy-start | bytes 7077892
  177.6 3.8 %copy-start.2 = (bf16[128,768]{1,0:T(8,128)(2,1)S(1)}, bf16[128,768]{1,0:T(8,128)(2,1)}, u32[]{:S(2)}) copy-start(bf16[128,768]{1,0:T(8,128)(2,1)} %get-tuple-element.20) | copy-start | bytes 589828
  179.7 2.4 %copy-start.1 = (f32[128,768]{1,0:T(8,128)S(1)}, f32[128,768]{1,0:T(8,128)}, u32[]{:S(2)}) copy-start(f32[128,768]{1,0:T(8,128)} %get-tuple-element.21) | copy-start | bytes 1179652
  179.7 3.1 %copy-start.4 = (f32[3,2,192]{2,1,0:T(2,128)S(1)}, f32[3,2,192]{2,1,0:T(2,128)}, u32[]{:S(2)}) copy-start(f32[3,2,192]{2,1,0:T(2,128)} %get-tuple-element.24) | copy-start | bytes 13828

commit v5 on v4

--- a/solution.py
+++ b/solution.py
@@ -441,7 +441,10 @@
 
 
 FF1, AT1, FF0, AT0 = ("ff", 1), ("at", 1), ("ff", 0), ("at", 0)
-PLAN = {1: {1: (FF1,), 4: (FF1,), 7: (FF1,), 8: (AT1,)}, 0: {0: (FF1,), 1: (AT1, FF0), 4: (FF1, AT1, FF0), 5: (AT0,), 7: (FF1, AT1, FF0)}}
+PLAN = {
+    1: {1: (FF1,), 4: (FF1,), 7: (FF1,), 8: (AT1,)},
+    0: {0: (FF1,), 1: (AT1, FF0), 4: (FF1, AT1, FF0), 5: (AT0,), 7: (AT0, FF1, AT1, FF0)},
+}
 
 
 def step_kernel(

time: 184 us -> 182 us (0.989)
  Pallas kernels: 168 us -> 166 us
    pallas_call x1, Pallas kernels: 168 us -> 166 us  [whole_step(): pl.pallas_call(step_kernel, name='training_step', out_shape=[jax.ShapeDty...]
where the time goes in v5:
time: 182 us; the launch traced here: 181 us
  Pallas kernels  166 us (91%)
  other arithmetic  11 us (6%)
  local copies, waits for them, and re-layouts  4.13 us (2%)
    pallas_call x1, Pallas kernels, whole_step(): pl.pallas_call(step_kernel, name='training_step', out_shape=[jax.ShapeDty...  166 us
    convert_element_type x1, other arithmetic, on_device(): ff[:, D:].astype(F32)  7.09 us

profile of v5, /device:TPU:0, one launch (start us, length us, event | category | flops | bytes accessed | tf_op | source)
XLA Modules:
  0.0 181.5 jit_solution(309767034079361895)
XLA Ops:
  0.7 0.1 multiply_cosine_fusion
  0.8 0.6 pad_maximum_fusion.rot_ref
  1.4 165.6 %training_step.1 = (bf16[128,768]{1,0:T(8,128)(2,1)}, f32[128,768]{1,0:T(8,128)}, bf16[2,1536,768]{2,1,0:T(8,128)(2,1)}, bf16[2,768,768]{2,1,0:T(8,128)(2,1)}, f...) custom-call(bf16[128,768]{1,0:T(8,128)(2,1)} %bitcast.29, bf16[128,768]{1,0:T(8,128)(2,1)} %bitcast.30, bf16[2,768]{1,0:T(2,128)(2,1)} %g1_ref.1, ...), custom_call_target="tpu_custom_call" | custom-call | tf_op jit(solution)/shard_map/training_step/pallas_call | solution.py:925
  167.0 1.4 slice_bitcast_fusion
  168.4 0.0 copy-start.3
  168.4 0.0 copy-start
  168.4 7.1 %slice_convert_fusion = (f32[2,768,768]{2,1,0:T(8,128)}, f32[2,768,768]{2,1,0:T(8,128)}) fusion(bf16[2,1536,768]{2,1,0:T(8,128)(2,1)} %get-tuple-element.25), kind=kLoop, calls=%fused_computation.1 | loop fusion | flops 2359296 | bytes 14155776 | tf_op jit(solution)/shard_map/convert_element_type | solution.py:996
  175.5 0.0 copy-done
  175.5 0.1 slice.35
  175.6 0.0 copy-start.2
  175.7 2.1 %convert_bitcast_fusion = f32[2,768,3,192]{1,3,2,0:T(8,128)} fusion(bf16[2,3,192,768]{3,2,1,0:T(8,128)(2,1)S(1)} %bitcast.25), kind=kLoop, calls=%fused_computation | loop fusion | flops 884736 | bytes 5308416 | tf_op jit(solution)/shard_map/transpose | solution.py:990
  177.8 0.0 copy-start.1
  177.8 0.0 copy-start.4
  177.8 1.1 slice_convert_fusion.2
  178.9 0.0 copy-done.3
  178.9 0.6 copy.32
  179.5 0.0 copy-done.2
  179.5 0.7 copy.33
  180.1 0.0 copy-done.1
  180.1 0.7 copy.34
  180.9 0.0 copy-done.4
  180.9 0.6 copy.35
  (2 shorter events, 0.0 us)
Async XLA Ops:
  168.4 10.4 %copy-start.3 = (f32[2,768]{1,0:T(2,128)}, f32[2,768]{1,0:T(2,128)S(1)}, u32[]{:S(2)}) copy-start(f32[2,768]{1,0:T(2,128)S(1)} %get-tuple-element.87) | copy-start | bytes 18436
  168.4 7.1 %copy-start = (bf16[2,768,768]{2,1,0:T(8,128)(2,1)S(1)}, bf16[2,768,768]{2,1,0:T(8,128)(2,1)}, u32[]{:S(2)}) copy-start(bf16[2,768,768]{2,1,0:T(8,128)(2,1)} %get-tuple-element.23) | copy-start | bytes 7077892
  175.6 3.8 %copy-start.2 = (bf16[128,768]{1,0:T(8,128)(2,1)S(1)}, bf16[128,768]{1,0:T(8,128)(2,1)}, u32[]{:S(2)}) copy-start(bf16[128,768]{1,0:T(8,128)(2,1)} %get-tuple-element.20) | copy-start | bytes 589828
  177.8 2.4 %copy-start.1 = (f32[128,768]{1,0:T(8,128)S(1)}, f32[128,768]{1,0:T(8,128)}, u32[]{:S(2)}) copy-start(f32[128,768]{1,0:T(8,128)} %get-tuple-element.21) | copy-start | bytes 1179652
  177.8 3.1 %copy-start.4 = (f32[3,2,192]{2,1,0:T(2,128)S(1)}, f32[3,2,192]{2,1,0:T(2,128)}, u32[]{:S(2)}) copy-start(f32[3,2,192]{2,1,0:T(2,128)} %get-tuple-element.24) | copy-start | bytes 13828
